TPU v7x, 512 devices: a whole 4x8x8 slice. The times are simulated.
512 devices in a mesh: group: 16 (over z_lo, x, core), shard: 32 (over z_hi, y).
Axes of the slice: x: 4, y: 8, z: 8 (z_hi: 4, z_lo: 2; z = z_hi * 2 + z_lo), core: 2. Of those that a mesh axis runs over, the one named last changes fastest.
Arguments:
- master_new: float32 [32, 96, 128, 128], P('shard', 'group'), may hold values from -60 to 60
- sent_base: bfloat16 [32, 96, 128, 128], P('shard', 'group'), may hold values from -6 to 6
- rollout_base: bfloat16 [12288, 2048], P('shard'), may hold values from -6 to 6
- tokens: bfloat16 [16, 32, 256, 2048], P('group', 'shard'), may hold values from -0.13183594 to 0.13183594
- lengths: int32 [32, 16], replicated, may hold values from 1 to 6, 48 in all within a row
- expert_slot: int32 [8], replicated, may hold values from 0 to 7, each once
Outputs:
- new_weights: bfloat16 [12288, 2048], P('shard')
- in_flight: bfloat16 [16, 32, 256, 384], P('group', 'shard')
Inputs may be any that keep to these rules, and one draw needn't show every extreme that they name: `lengths`: row s splits column s's 48 tiles among the 16 groups; each row sums to 48 and its largest entry is 6. `expert_slot`: a permutation of the 8 slots.
All inputs are finite; a program needn't handle non-finite values.
Results may differ from a plain program's by a relative error of at most 0.0051.
Values may be sent and summed in bfloat16 or wider, within the bound.
No kernel may reach another device: no remote copies, remote signals or barrier semaphores. Data moves between devices by JAX's collectives and lax.ppermute only.
A program may use at most 64 MiB of HBM per device.

v0:
```python
import jax
import jax.numpy as jnp
from jax import lax
from jax.sharding import PartitionSpec as P

MI = 1536
TPW = 4


CLIP_RATIO = 2.5
EPSILON = 1e-06


def encode(master, previous):
    change = master - previous.astype(jnp.float32)
    tile_scale = jnp.sqrt(jnp.mean(change * change, axis=(-2, -1)) + EPSILON).astype(jnp.bfloat16)
    tile_scale = lax.optimization_barrier(tile_scale)
    widened = tile_scale.astype(jnp.float32)[..., None, None]
    encoded = jnp.clip(change / widened, -CLIP_RATIO, CLIP_RATIO).astype(jnp.bfloat16)
    return (encoded, tile_scale)


def decode(encoded, tile_scale):
    encoded = lax.optimization_barrier(encoded)
    return encoded.astype(jnp.float32) * tile_scale.astype(jnp.float32)[..., None, None]


def shards(master_new, sent_base, rollout_base, tokens, lengths, expert_slot):
    n_group = lax.axis_size("group")
    n_shard = lax.axis_size("shard")
    most_slots = master_new.shape[1]
    block_edge = master_new.shape[2]
    rows_dev = rollout_base.shape[0]
    feature_width = rollout_base.shape[1]
    tile_rows = MI // block_edge
    tile_cols = feature_width // block_edge
    rows_each = rows_dev // block_edge
    experts = n_shard // TPW
    pairs_each = tile_cols // TPW
    per_stretch = rows_each * tile_cols
    capacity = rows_each * max(1, pairs_each // experts)
    column = lax.axis_index("shard")
    in_flight = lax.dot_general(
        tokens[0, 0], rollout_base, (((1,), (1,)), ((), ())), preferred_element_type=jnp.float32
    ).astype(jnp.bfloat16)[None, None]
    encoded, tile_scale = encode(master_new[0], sent_base[0])
    gathered, gathered_scale = (
        lax.all_gather(encoded, "group", axis=0, tiled=True),
        lax.all_gather(tile_scale, "group", axis=0, tiled=True),
    )
    my_lengths = lax.dynamic_index_in_dim(lengths, column, 0, keepdims=False)
    run_ends = jnp.cumsum(my_lengths)
    starts = run_ends - my_lengths
    positions = jnp.arange(per_stretch, dtype=jnp.int32)
    owners = jnp.sum((run_ends[None, :] <= positions[:, None]).astype(jnp.int32), axis=1)
    group_ids = jnp.arange(n_group, dtype=jnp.int32)
    owner_start = jnp.sum(
        jnp.where(owners[:, None] == group_ids[None, :], starts[None, :], 0), axis=1
    )
    sources = owners * most_slots + positions - owner_start
    stretch_tiles = gathered[sources]
    stretch_scale = gathered_scale[sources]
    flat_index = column * per_stretch + positions
    pair_index = flat_index // tile_rows
    row_tile = flat_index % tile_rows
    expert = pair_index % experts
    expert_ids = jnp.arange(experts, dtype=jnp.int32)
    slot_of = jnp.sum(
        jnp.where(expert[:, None] == expert_ids[None, :], expert_slot[None, :], 0), axis=1
    )
    target = slot_of * TPW + row_tile // rows_each
    within = (pair_index - column * pairs_each) // experts * rows_each + row_tile % rows_each
    send_index = target * capacity + within
    my_slot = column // TPW
    my_expert = jnp.sum(jnp.where(expert_slot == my_slot, expert_ids, 0))
    senders = jnp.arange(n_shard, dtype=jnp.int32)[:, None]
    slot_rank = jnp.arange(capacity, dtype=jnp.int32)[None, :]
    first_pair = senders * pairs_each
    leading = first_pair + jnp.mod(my_expert - first_pair, experts)
    pair_recv = leading + slot_rank // rows_each * experts
    present = pair_recv < first_pair + pairs_each
    local_index = jnp.where(
        present, slot_rank % rows_each * tile_cols + pair_recv // experts, per_stretch
    )
    local_index = local_index.reshape(-1)
    total_slots = n_shard * capacity
    stretch_update = decode(stretch_tiles, stretch_scale)
    outgoing = (
        jnp.zeros((total_slots, block_edge, block_edge), jnp.float32)
        .at[send_index]
        .set(stretch_update)
    )
    incoming = lax.all_to_all(outgoing, "shard", split_axis=0, concat_axis=0, tiled=True)
    update = (
        jnp.zeros((per_stretch, block_edge, block_edge), jnp.float32)
        .at[local_index]
        .set(incoming, mode="drop")
    )
    weight_tiles = update.reshape(rows_each, tile_cols, block_edge, block_edge).transpose(
        0, 2, 1, 3
    )
    weight_tiles = weight_tiles.reshape(rows_dev, feature_width)
    new_weights = (rollout_base.astype(jnp.float32) + weight_tiles).astype(jnp.bfloat16)
    return (new_weights, in_flight)


def solution(mesh):
    placed = (
        P("shard", "group", None, None),
        P("shard", "group", None, None),
        P("shard", None),
        P("group", "shard", None, None),
        P(),
        P(),
    )
    return jax.shard_map(
        shards,
        mesh=mesh,
        in_specs=placed,
        out_specs=(P("shard", None), P("group", "shard", None, None)),
        check_vma=False,
    )
```

profile of v0, /device:TPU:165, one launch (start us, length us, event | category | flops | bytes accessed | tf_op | source)
XLA Modules:
  0.0 340.6 jit_solution(2516548034433600460)
XLA Ops:
  7.2 1.3 fusion.3
  8.5 1.8 fusion.5
  10.4 0.8 constant_dynamic-slice_fusion
  11.4 0.1 reduce
  11.5 1.3 dynamic-slice
  13.4 0.2 dynamic-update-slice
  13.7 23.6 %all-reduce = bf16[96]{0:T(256)(128)(2,1)S(1)} all-reduce(bf16[96]{0:T(256)(128)(2,1)S(1)} %dynamic-update-slice), channel_id=1, replica_groups=mesh['group'=16,'shard'=32] {'group'}, use_global_device_ids=true, to_apply=%add | all-reduce | flops 96 | bytes 384
  37.4 0.8 gather_fusion.1
  38.2 0.7 select_reduce_fusion.1
  39.0 15.3 %all-gather.2.cloned.1.call-done = bf16[96,128,128]{2,1,0:T(8,128)(2,1)} async-done(((bf16[6,128,128]{2,1,0:T(8,128)(2,1)}), bf16[96,128,128]{2,1,0:T(8,128)(2,1)}) %all-gather.2.cloned.1.call-update) | async-done | bytes 3145744 | tf_op jit(solution)/shard_map/all_gather | solution.py:48
  54.3 2.7 gather_fusion
  57.0 1.9 convert_multiply_fusion
  59.0 3.4 %broadcast_in_dim.62 = f32[96,128,128]{2,1,0:T(8,128)} broadcast(f32[]{:T(128)} %constant.114.clone.1), dimensions={} | broadcast | bytes 6291460 | tf_op jit(solution)/shard_map/broadcast_in_dim | solution.py:89
  62.4 9.1 %scatter_fusion = f32[96,128,128]{2,1,0:T(8,128)} fusion(f32[96,128,128]{2,1,0:T(8,128)} %broadcast_in_dim.62, s32[48]{0:T(128)S(1)} %fusion.13, f32[48,128,128]{2,1,0:T(8,128)} %convert_multiply_fusion), kind=kCustom, calls=%fused_computation.2 | custom fusion | bytes 9437376 | tf_op jit(solution)/shard_map/scatter | solution.py:91
  71.5 11.6 %all-to-all-start = ((f32[96,128,128]{2,1,0:T(8,128)}), f32[96,128,128]{2,1,0:T(8,128)}, u32[]{:S(2)}, u32[]{:S(2)}) async-start(f32[96,128,128]{2,1,0:T(8,128)} %scatter_fusion), calls=%async_computation | async-start | bytes 12582912 | tf_op jit(solution)/shard_map/all_to_all | solution.py:93
  83.2 0.6 fusion.10
  83.8 0.7 fusion.6
  84.9 0.1 lt.78
  85.0 1.4 fusion.1
  86.4 222.0 %all-to-all-done = f32[96,128,128]{2,1,0:T(8,128)} async-done(((f32[96,128,128]{2,1,0:T(8,128)}), f32[96,128,128]{2,1,0:T(8,128)}, u32[]{:S(2)}, u32[]{:S(2)}) %all-to-all-start) | async-done | bytes 6291488 | tf_op jit(solution)/shard_map/all_to_all | solution.py:93
  308.5 2.1 broadcast_in_dim.59
  310.6 17.1 %scatter_fusion.1 = f32[48,128,128]{2,1,0:T(8,128)} fusion(f32[48,128,128]{2,1,0:T(8,128)} %broadcast_in_dim.59, s32[96]{0:T(128)S(1)} %fusion.18, f32[96,128,128]{2,1,0:T(8,128)} %all-to-all-done), kind=kCustom, calls=%fused_computation.3 | custom fusion | bytes 18874752 | tf_op jit(solution)/shard_map/scatter | solution.py:97
  327.6 3.7 %copy.20 = f32[3,128,16,128]{3,2,1,0:T(8,128)S(1)} copy(f32[3,128,16,128]{3,1,2,0:T(8,128)} %bitcast.54) | data formatting | bytes 6291456 | tf_op jit(solution)/shard_map/transpose | solution.py:99
  331.3 2.4 fusion
  (31 shorter events, 0.9 us)
Async XLA Ops:
  7.2 77.9 %copy-start = (bf16[1,1,256,2048]{3,2,1,0:T(8,128)(2,1)S(1)}, bf16[1,1,256,2048]{3,2,1,0:T(8,128)(2,1)}, u32[]{:S(2)}) copy-start(bf16[1,1,256,2048]{3,2,1,0:T(8,128)(2,1)} %param.9) | copy-start | bytes 3145732
  7.2 47.1 %all-gather.2.cloned.1.call-start = ((), (), s32[]{:S(2)}) async-start(), calls=%async_computation.1 | async-start | bytes 3342336 | tf_op jit(solution)/shard_map/all_gather | solution.py:48
  71.5 11.7 %copy-start.2 = (s32[8]{0:T(128)S(1)}, s32[8]{0:T(128)}, u32[]{:S(2)}) copy-start(s32[8]{0:T(128)} %param.11) | copy-start | bytes 100
  71.5 13.5 %copy-start.1 = (bf16[384,2048]{1,0:T(8,128)(2,1)S(1)}, bf16[384,2048]{1,0:T(8,128)(2,1)}, u32[]{:S(2)}) copy-start(bf16[384,2048]{1,0:T(8,128)(2,1)} %param.8) | copy-start | bytes 4718596
  71.5 237.0 %all-to-all-start = ((f32[96,128,128]{2,1,0:T(8,128)}), f32[96,128,128]{2,1,0:T(8,128)}, u32[]{:S(2)}, u32[]{:S(2)}) async-start(f32[96,128,128]{2,1,0:T(8,128)} %scatter_fusion), calls=%async_computation | async-start | bytes 12582912 | tf_op jit(solution)/shard_map/all_to_all | solution.py:93
Sparse Core Ops, SparseCore 0:
  10.7 43.5 all-gather.1
where the time goes:
time: 341 us
  waiting for transfers between devices  237 us (70%)
  local copies, waits for them, and re-layouts  41.8 us (12%)
  blocking collectives  23.6 us (7%)
  between operations  14.8 us (4%)
  starting transfers between devices  11.7 us (3%)
  other arithmetic  10 us (3%)
    all_to_all x1, waiting for transfers between devices, shards(): lax.all_to_all(outgoing, 'shard', split_axis=0, concat_axis=0, tiled=True)  222 us
    unnamed x1, blocking collectives  23.6 us
    scatter x1, local copies, waits for them, and re-layouts, shards(): update = jnp.zeros((per_stretch, block_edge, block_edge), jnp.float32).at...  17.1 us
    all_gather x1, waiting for transfers between devices, shards(): lax.all_gather(encoded, 'group', axis=0, tiled=True)  15.3 us
    all_to_all x1, starting transfers between devices, shards(): lax.all_to_all(outgoing, 'shard', split_axis=0, concat_axis=0, tiled=True)  11.6 us
    scatter x1, local copies, waits for them, and re-layouts, shards(): outgoing = jnp.zeros((total_slots, block_edge, block_edge), jnp.float32)....  9.11 us
  transfers between devices with their start and end apart: 2, of which 2 were waited for; matrix products, arithmetic and copies ran while one was open for 2% of the time, Pallas kernels for 0%

commit v1 on v0

v1 whole, which is shorter than its diff:
```python
import jax
import jax.numpy as jnp
from jax import lax
from jax.experimental import pallas as pl
from jax.experimental.pallas import tpu as pltpu
from jax.sharding import Mesh
from jax.sharding import PartitionSpec as P

CLIP_RATIO = 2.5
EPSILON = 1e-06

BLK = 128
HALF = 4
TROWS = 12
MOST = 6
GROUPS = 16


def place():
    zl, x, c = lax.axis_index("zl"), lax.axis_index("x"), lax.axis_index("c")
    zh, y = lax.axis_index("zh"), lax.axis_index("y")
    return zl, x, c, zh, y


def mod16(v):
    return lax.bitwise_and(v, 15)


def encode_kernel(lengths, master, sent, out):
    zl, x, c, zh, y = place()
    g, s = zl * 8 + x * 2 + c, zh * 8 + y
    start = jnp.int32(0)
    for i in range(GROUPS):
        start += jnp.where(i < g, lengths[s, i], 0)
    count = lengths[s, g]
    for j in range(MOST):
        change = master[0, j] - sent[0, j].astype(jnp.float32)
        mean = jnp.sum(change * change, axis=(0, 1), keepdims=True) * (1.0 / (BLK * BLK))
        scale = jnp.sqrt(mean + EPSILON).astype(jnp.bfloat16).astype(jnp.float32)
        encoded = jnp.clip(change / scale, -CLIP_RATIO, CLIP_RATIO).astype(jnp.bfloat16)
        value = (encoded.astype(jnp.float32) * scale).astype(jnp.bfloat16)

        @pl.when(j < count)
        def _():
            out[mod16(start + j + 4 * (y // 2) + zh)] = value


def to_y_kernel(lengths, slots, got, out):
    zl, x, c, zh, y = place()
    g, s = zl * 8 + x * 2 + c, zh * 8 + y
    first = mod16(g - 4 * (y // 2) - zh + 32)
    owners = [jnp.int32(0)] * 3
    end = jnp.int32(0)
    for i in range(GROUPS - 1):
        end += lengths[s, i]
        for m in range(3):
            owners[m] += jnp.where(end <= first + 16 * m, 1, 0)
    for m in range(3):
        q = first + 16 * m
        slot = slots[HALF * (y % 2) + q // TROWS]
        out[(slot % 2) * 4 + (q % TROWS) // 3] = got[owners[m]]


def expert_at(slots, p):
    e = jnp.int32(0)
    for i in range(2 * HALF):
        e += jnp.where(slots[i] == p, i, 0)
    return e


def to_z_kernel(slots, got, out):
    zl, x, c, zh, y = place()
    g = zl * 8 + x * 2 + c
    for to in range(4):
        e = expert_at(slots, 2 * to + y // 4)
        u = mod16(g - 12 * (e % HALF) - 3 * (y % 4) - zh + 64)
        tile = got[(u // 4) * 2 + e // HALF]
        out[2 * to] = tile
        out[2 * to + 1] = tile


def hole(x, c, y):
    return lax.bitwise_and(2 * x + c - 3 * (y % 4) - 3 + 16, 3)


def to_x_kernel(got, out):
    zl, x, c, zh, y = place()
    skip = hole(x, c, y)
    for a in range(3):
        at = lax.bitwise_and(skip + 1 + a, 3)
        for lo in range(2):
            tile = got[at * 2 + lo]
            for to in range(4):
                out[to * 6 + a * 2 + lo] = tile


def add_kernel(slots, mine, other, base, out):
    zl, x, c, zh, y = place()
    e4 = expert_at(slots, 2 * zh + y // 4) % HALF
    for i in range(3):
        for col in range(16):
            from_zh = col // 4
            g = mod16(i + 4 * (col % 4) + 12 * e4 + 3 * (y % 4) + from_zh)
            from_zl, from_x, from_c = g // 8, (g // 2) % 4, g % 2
            a = lax.bitwise_and(from_zh - hole(from_x, from_c, y) - 1 + 8, 3)
            n = from_x * 6 + a * 2 + from_zl
            tile = jnp.where(from_c == c, mine[n], other[n]).astype(jnp.float32)
            rows, cols = pl.ds(i * BLK, BLK), pl.ds(col * BLK, BLK)
            out[rows, cols] = (base[rows, cols].astype(jnp.float32) + tile).astype(jnp.bfloat16)


SMEM = pl.BlockSpec(memory_space=pltpu.SMEM)
VMEM = pl.BlockSpec(memory_space=pltpu.VMEM)
LIMIT = pltpu.CompilerParams(vmem_limit_bytes=32 * 1024 * 1024)


def tiles_call(kernel, n, name, specs, *args):
    return pl.pallas_call(
        kernel,
        out_shape=jax.ShapeDtypeStruct((n, BLK, BLK), jnp.bfloat16),
        in_specs=specs,
        out_specs=VMEM,
        compiler_params=LIMIT,
        name=name,
    )(*args)


def exchange(x, axes):
    return lax.all_to_all(x, axes, split_axis=0, concat_axis=0, tiled=True)


def shards(master_new, sent_base, rollout_base, tokens, lengths, expert_slot):
    sent = tiles_call(encode_kernel, 16, "encode", [SMEM, VMEM, VMEM], lengths, master_new, sent_base)
    home = exchange(sent, ("zl", "x", "c"))
    by_y = tiles_call(to_y_kernel, 8, "to_y", [SMEM, SMEM, VMEM], lengths, expert_slot, home)
    by_y = exchange(by_y, ("y",))
    by_z = tiles_call(to_z_kernel, 8, "to_z", [SMEM, VMEM], expert_slot, by_y)
    by_z = exchange(by_z, ("zh", "zl"))
    by_x = tiles_call(to_x_kernel, 24, "to_x", [VMEM], by_z)
    mine = exchange(by_x, ("x",))
    other = lax.ppermute(mine, "c", [(0, 1), (1, 0)])
    in_flight = lax.dot_general(
        tokens[0, 0], rollout_base, (((1,), (1,)), ((), ())), preferred_element_type=jnp.float32
    ).astype(jnp.bfloat16)[None, None]
    new_weights = pl.pallas_call(
        add_kernel,
        out_shape=jax.ShapeDtypeStruct(rollout_base.shape, jnp.bfloat16),
        in_specs=[SMEM, VMEM, VMEM, VMEM],
        out_specs=VMEM,
        compiler_params=LIMIT,
        name="add",
    )(expert_slot, mine, other, rollout_base)
    return (new_weights, in_flight)


def solution(mesh):
    fine = Mesh(mesh.devices.reshape(2, 4, 2, 4, 8), ("zl", "x", "c", "zh", "y"))
    group, shard = ("zl", "x", "c"), ("zh", "y")
    placed = (
        P(shard, group, None, None),
        P(shard, group, None, None),
        P(shard, None),
        P(group, shard, None, None),
        P(),
        P(),
    )
    return jax.shard_map(
        shards,
        mesh=fine,
        in_specs=placed,
        out_specs=(P(shard, None), P(group, shard, None, None)),
        check_vma=False,
    )
```

time: 341 us -> 85.2 us (0.25)
  the two profiles are of different devices: /device:TPU:165 before, /device:TPU:1 now
where the time goes in v1:
time: 85.2 us; the launch traced here: 84.9 us
  blocking collectives  68 us (80%)
  Pallas kernels  6.03 us (7%)
  starting transfers between devices  5.44 us (6%)
  local copies, waits for them, and re-layouts  2.81 us (3%)
  matrix products  1.41 us (2%)
    all_to_all x4, blocking collectives, exchange(): return lax.all_to_all(x, axes, split_axis=0, concat_axis=0, tiled=True)  68 us
    ppermute x1, starting transfers between devices, shards(): other = lax.ppermute(mine, 'c', [(0, 1), (1, 0)])  5.44 us
    pallas_call x4, Pallas kernels, tiles_call(): pl.pallas_call(kernel, out_shape=jax.ShapeDtypeStruct((n, BLK, BLK), jnp....  3.48 us
    unnamed x11, local copies, waits for them, and re-layouts  2.81 us
    pallas_call x1, Pallas kernels, shards(): pl.pallas_call(add_kernel, out_shape=jax.ShapeDtypeStruct(rollout_base.sh...  2.55 us
  transfers between devices with their start and end apart: 1, of which 1 were waited for; matrix products, arithmetic and copies ran while one was open for 2% of the time, Pallas kernels for 0%

profile of v1, /device:TPU:1, one launch (start us, length us, event | category | flops | bytes accessed | tf_op | source)
XLA Modules:
  0.0 84.9 jit_solution(17253772306560023797)
XLA Ops:
  0.6 0.0 copy-start
  0.6 0.0 copy-start.4
  0.7 0.9 %copy.9.lengths = s32[32,16]{1,0:T(8,128)S(1)} copy(s32[32,16]{0,1:T(8,128)} %param.10) | data formatting | bytes 4096 | tf_op args[4]
  1.5 0.0 copy-start.2
  1.5 1.0 %copy-done.2 = f32[1,6,128,128]{3,2,1,0:T(8,128)S(1)} copy-done((f32[1,6,128,128]{3,2,1,0:T(8,128)S(1)}, f32[1,6,128,128]{3,2,1,0:T(8,128)}, u32[]{:S(2)}) %copy-start.2) | copy-done | bytes 393240
  2.5 0.0 copy-start.3
  2.5 0.9 %copy-done.3 = bf16[1,6,128,128]{3,2,1,0:T(8,128)(2,1)S(1)} copy-done((bf16[1,6,128,128]{3,2,1,0:T(8,128)(2,1)S(1)}, bf16[1,6,128,128]{3,2,1,0:T(8,128)(2,1)}, u32[]{:S(2)}) %copy-start.3) | copy-done | bytes 196632
  3.4 1.8 %encode.1 = bf16[16,128,128]{2,1,0:T(8,128)(2,1)S(1)} custom-call(s32[32,16]{1,0:T(8,128)S(1)} %copy.9.lengths, f32[1,6,128,128]{3,2,1,0:T(8,128)S(1)} %copy-done.2, bf16[1,6,128,128]{3,2,1,0:T(8,128)(2,1)S(1)} %copy-done.3), custom_call_target="tpu_custom_call" | custom-call | tf_op jit(solution)/shard_map/encode/pallas_call | solution.py:118
  5.2 19.2 %all_to_all.20.got = bf16[16,128,128]{2,1,0:T(8,128)(2,1)S(1)} all-to-all(bf16[16,128,128]{2,1,0:T(8,128)(2,1)S(1)} %encode.1), channel_id=1, replica_groups=mesh['zl'=2,'x'=4,'c'=2,'zh'=4,'y'=8] {'zl','x','c'}, dimensions={0} | all-to-all | bytes 1048576 | tf_op jit(solution)/shard_map/all_to_all | solution.py:129
  24.4 0.0 copy-done.4
  24.4 0.9 %to_y.1 = bf16[8,128,128]{2,1,0:T(8,128)(2,1)S(1)} custom-call(s32[32,16]{1,0:T(8,128)S(1)} %copy.9.lengths, s32[8]{0:T(128)S(1)} %copy-done.4, bf16[16,128,128]{2,1,0:T(8,128)(2,1)S(1)} %all_to_all.20.got), custom_call_target="tpu_custom_call" | custom-call | tf_op jit(solution)/shard_map/to_y/pallas_call | solution.py:118
  25.4 14.7 %all_to_all.21.got = bf16[8,128,128]{2,1,0:T(8,128)(2,1)S(1)} all-to-all(bf16[8,128,128]{2,1,0:T(8,128)(2,1)S(1)} %to_y.1), channel_id=1, replica_groups=mesh['zl'=2,'x'=4,'c'=2,'zh'=4,'y'=8] {'y'}, dimensions={0} | all-to-all | bytes 524288 | tf_op jit(solution)/shard_map/all_to_all | solution.py:129
  40.1 0.7 to_z.1
  40.8 0.0 copy-start.1
  40.8 18.5 %all_to_all.22.got = bf16[8,128,128]{2,1,0:T(8,128)(2,1)S(1)} all-to-all(bf16[8,128,128]{2,1,0:T(8,128)(2,1)S(1)} %to_z.1), channel_id=1, replica_groups=mesh['zl'=2,'x'=4,'c'=2,'zh'=4,'y'=8] {'zh','zl'}, dimensions={0} | all-to-all | bytes 524288 | tf_op jit(solution)/shard_map/all_to_all | solution.py:129
  59.3 0.1 to_x.1
  59.4 15.6 %all_to_all.23.mine = bf16[24,128,128]{2,1,0:T(8,128)(2,1)S(1)} all-to-all(bf16[24,128,128]{2,1,0:T(8,128)(2,1)S(1)} %to_x.1), channel_id=1, replica_groups=mesh['zl'=2,'x'=4,'c'=2,'zh'=4,'y'=8] {'x'}, dimensions={0} | all-to-all | bytes 1572864 | tf_op jit(solution)/shard_map/all_to_all | solution.py:129
  75.0 5.4 %collective-permute-start = (bf16[24,128,128]{2,1,0:T(8,128)(2,1)S(1)}, bf16[24,128,128]{2,1,0:T(8,128)(2,1)S(1)}, u32[]{:S(2)}, u32[]{:S(2)}) collective-permute-start(bf16[24,128,128]{2,1,0:T(8,128)(2,1)S(1)} %all_to_all.23.mine), channel_id=1, source_target_pairs={{0,32},{32,0},{1,33},{33,1},{2,34},{34,2},{3,35},{35,3},{4,36},{36... | collective-permute-start | bytes 2359304 | tf_op jit(solution)/shard_map/ppermute | solution.py:141
  80.4 0.0 copy-done
  80.4 0.0 copy-done.1
  80.4 1.4 %fusion = bf16[1,1,256,384]{3,2,1,0:T(8,128)(2,1)} fusion(bf16[384,2048]{1,0:T(8,128)(2,1)S(1)} %copy-done.1, bf16[1,1,256,2048]{3,2,1,0:T(8,128)(2,1)S(1)} %copy-done), kind=kOutput, calls=%fused_computation.1 | convolution fusion | flops 402751488 | bytes 2818048 | tf_op jit(solution)/shard_map/dot_general | solution.py:142
  81.9 0.5 collective-permute-done.other
  82.3 2.6 %add.1 = bf16[384,2048]{1,0:T(8,128)(2,1)} custom-call(s32[8]{0:T(128)S(1)} %copy-done.4, bf16[24,128,128]{2,1,0:T(8,128)(2,1)S(1)} %all_to_all.23.mine, bf16[24,128,128]{2,1,0:T(8,128)(2,1)S(1)} %collective-permute-done.other, bf16[384,2048]{1,0:T(8,128)(2,1)S(1)} %copy-done.1), custom_call_target="tpu_custom_call" | custom-call | tf_op jit(solution)/shard_map/add/pallas_call | solution.py:145
Async XLA Ops:
  0.6 79.8 %copy-start = (bf16[1,1,256,2048]{3,2,1,0:T(8,128)(2,1)S(1)}, bf16[1,1,256,2048]{3,2,1,0:T(8,128)(2,1)}, u32[]{:S(2)}) copy-start(bf16[1,1,256,2048]{3,2,1,0:T(8,128)(2,1)} %param.9) | copy-start | bytes 3145732
  0.6 23.8 %copy-start.4 = (s32[8]{0:T(128)S(1)}, s32[8]{0:T(128)}, u32[]{:S(2)}) copy-start(s32[8]{0:T(128)} %slots.5) | copy-start | bytes 100
  1.5 1.0 %copy-start.2 = (f32[1,6,128,128]{3,2,1,0:T(8,128)S(1)}, f32[1,6,128,128]{3,2,1,0:T(8,128)}, u32[]{:S(2)}) copy-start(f32[1,6,128,128]{3,2,1,0:T(8,128)} %master.1) | copy-start | bytes 1179652
  2.5 0.9 %copy-start.3 = (bf16[1,6,128,128]{3,2,1,0:T(8,128)(2,1)S(1)}, bf16[1,6,128,128]{3,2,1,0:T(8,128)(2,1)}, u32[]{:S(2)}) copy-start(bf16[1,6,128,128]{3,2,1,0:T(8,128)(2,1)} %sent.1) | copy-start | bytes 589828
  40.8 39.7 %copy-start.1 = (bf16[384,2048]{1,0:T(8,128)(2,1)S(1)}, bf16[384,2048]{1,0:T(8,128)(2,1)}, u32[]{:S(2)}) copy-start(bf16[384,2048]{1,0:T(8,128)(2,1)} %base.1) | copy-start | bytes 4718596
  75.0 7.3 %collective-permute-start = (bf16[24,128,128]{2,1,0:T(8,128)(2,1)S(1)}, bf16[24,128,128]{2,1,0:T(8,128)(2,1)S(1)}, u32[]{:S(2)}, u32[]{:S(2)}) collective-permute-start(bf16[24,128,128]{2,1,0:T(8,128)(2,1)S(1)} %all_to_all.23.mine), channel_id=1, source_target_pairs={{0,32},{32,0},{1,33},{33,1},{2,34},{34,2},{3,35},{35,3},{4,36},{36... | collective-permute-start | bytes 2359304 | tf_op jit(solution)/shard_map/ppermute | solution.py:141

commit v2 on v1

v2 whole, which is shorter than its diff:
```python
import jax
import jax.numpy as jnp
import numpy as np
from jax import lax
from jax.experimental import pallas as pl
from jax.experimental.pallas import tpu as pltpu
from jax.sharding import Mesh
from jax.sharding import PartitionSpec as P

CLIP_RATIO = 2.5
EPSILON = 1e-06

AXES = {"zl": 2, "x": 4, "c": 2, "zh": 4, "ya": 2, "yb": 2, "yc": 2}
BLK = 128
HALF = 64
TROWS = 12
MOST = 6
GROUPS = 16
EXPERTS = 8


class Place:
    def __init__(self):
        at = {name: lax.axis_index(name) for name in AXES}
        self.c, self.zh, self.ya, self.yc = at["c"], at["zh"], at["ya"], at["yc"]
        self.g = at["zl"] * 8 + at["x"] * 2 + at["c"]
        self.cc = at["zh"] * 4 + at["ya"] * 2 + at["yb"]
        self.own = at["zh"] * 4 + at["yb"] * 2 + at["yc"]


def run_of(lengths, s, g):
    start = jnp.int32(0)
    for i in range(GROUPS):
        start += jnp.where(i < g, lengths[i, s], 0)
    return start, lengths[g, s]


def encode_kernel(lengths, master, sent, keep, give):
    at = Place()
    start, count = run_of(lengths, 2 * at.cc + at.yc, at.g)
    for j in range(MOST):
        change = master[0, j] - sent[0, j].astype(jnp.float32)
        mean = jnp.sum(change * change, axis=(0, 1), keepdims=True) * (1.0 / (BLK * BLK))
        scale = jnp.sqrt(mean + EPSILON).astype(jnp.bfloat16).astype(jnp.float32)
        encoded = jnp.clip(change / scale, -CLIP_RATIO, CLIP_RATIO).astype(jnp.bfloat16)
        value = (encoded.astype(jnp.float32) * scale).astype(jnp.bfloat16)
        r = lax.rem(start + j, TROWS)
        here = lax.bitwise_and(lax.bitwise_xor(lax.div(r, 3), at.cc), 1) == at.c

        @pl.when((j < count) & here)
        def _():
            keep[lax.rem(r, 3)] = value

        @pl.when((j < count) & jnp.logical_not(here))
        def _():
            give[lax.rem(r, 3)] = value


def home_kernel(lengths, slots, keep, got, out):
    at = Place()
    for tiles, g in ((keep, at.g), (got, lax.bitwise_xor(at.g, 1))):
        start, count = run_of(lengths, 2 * at.cc + at.yc, g)
        for j in range(MOST):
            q = lax.min(start + j, 47)
            r = lax.rem(q, TROWS)
            k, i = lax.div(r, 3), lax.rem(r, 3)
            p = slots[4 * at.yc + lax.div(q, TROWS)]
            home = lax.bitwise_xor(4 * lax.div(p, 2) + k, at.cc)

            @pl.when((j < count) & (lax.bitwise_and(home, 1) == at.c))
            def _():
                peer = lax.bitwise_and(home, 14)
                out[peer, i] = tiles[i, :HALF, :]
                out[peer + 1, i] = tiles[i, HALF:, :]


def part_kernel(lengths, slots, got, first, second):
    at = Place()
    m = lax.bitwise_xor(at.g, at.cc)
    k = lax.bitwise_and(m, 3)
    for part, out in ((at.yc, first), (1 - at.yc, second)):
        p = 2 * lax.div(m, 4) + part
        e = jnp.int32(0)
        for n in range(EXPERTS):
            e += jnp.where(slots[n] == p, n, 0)
        side = lax.div(e, 4)
        q = lax.rem(e, 4) * TROWS + 3 * k
        owners = [jnp.int32(0)] * 3
        end = jnp.int32(0)
        for n in range(GROUPS - 1):
            end += lengths[n, 2 * at.cc + side]
            for i in range(3):
                owners[i] += jnp.where(end <= q + i, 1, 0)
        for i in range(3):
            out[i] = got[lax.bitwise_and(owners[i], 14) + side, i]


def spread_kernel(first, second, out):
    at = Place()
    near = pl.ds(pl.multiple_of(at.ya * HALF, HALF), HALF)
    far = pl.ds(pl.multiple_of((1 - at.ya) * HALF, HALF), HALF)
    for i in range(3):
        for to in range(8):
            out[to, i, near, :] = first[i]
            out[to, i, far, :] = second[i]


def add_kernel(mine, other, base, out):
    at = Place()
    for col in range(16):
        g = lax.bitwise_xor(at.own, col)
        near = lax.bitwise_and(g, 1) == at.c
        chip = lax.div(g, 2)
        for i in range(3):
            tile = jnp.where(near, mine[chip, i], other[chip, i]).astype(jnp.float32)
            rows, cols = pl.ds(i * BLK, BLK), pl.ds(col * BLK, BLK)
            out[rows, cols] = (base[rows, cols].astype(jnp.float32) + tile).astype(jnp.bfloat16)


SMEM = pl.BlockSpec(memory_space=pltpu.SMEM)
VMEM = pl.BlockSpec(memory_space=pltpu.VMEM)


def call(kernel, name, specs, shapes, *args):
    outs = tuple(jax.ShapeDtypeStruct(s, jnp.bfloat16) for s in shapes)
    return pl.pallas_call(
        kernel,
        out_shape=outs,
        in_specs=specs,
        out_specs=(VMEM,) * len(outs),
        compiler_params=pltpu.CompilerParams(vmem_limit_bytes=32 * 1024 * 1024),
        name=name,
    )(*args)


def exchange(x, axes):
    return lax.all_to_all(x, axes, split_axis=0, concat_axis=0, tiled=True)


def routes(flip):
    sizes = tuple(AXES.values())
    pairs = []
    for n in range(512):
        zl, x, c, zh, ya, yb, yc = (int(v) for v in np.unravel_index(n, sizes))
        m = (zl * 8 + x * 2 + c) ^ (zh * 4 + ya * 2 + yb)
        to = (zl, x, c, m // 4, yc ^ flip, (m // 2) % 2, m % 2)
        pairs.append((n, int(np.ravel_multi_index(to, sizes))))
    return pairs


def shards(master_new, sent_base, rollout_base, tokens, lengths, expert_slot):
    lengths = lengths.T
    keep, give = call(
        encode_kernel, "encode", [SMEM, VMEM, VMEM], [(3, BLK, BLK)] * 2, lengths, master_new, sent_base
    )
    got = lax.ppermute(give, "c", [(0, 1), (1, 0)])
    (out,) = call(
        home_kernel, "home", [SMEM, SMEM, VMEM, VMEM], [(16, 3, HALF, BLK)], lengths, expert_slot, keep, got
    )
    home = exchange(out, ("zl", "x", "yc"))
    first, second = call(
        part_kernel, "part", [SMEM, SMEM, VMEM], [(3, HALF, BLK)] * 2, lengths, expert_slot, home
    )
    first = lax.ppermute(first, tuple(AXES), routes(0))
    second = lax.ppermute(second, tuple(AXES), routes(1))
    (out,) = call(spread_kernel, "spread", [VMEM, VMEM], [(8, 3, BLK, BLK)], first, second)
    mine = exchange(out, ("zl", "x"))
    other = lax.ppermute(mine, "c", [(0, 1), (1, 0)])
    in_flight = lax.dot_general(
        tokens[0, 0], rollout_base, (((1,), (1,)), ((), ())), preferred_element_type=jnp.float32
    ).astype(jnp.bfloat16)[None, None]
    (new_weights,) = call(
        add_kernel, "add", [VMEM, VMEM, VMEM], [rollout_base.shape], mine, other, rollout_base
    )
    return (new_weights, in_flight)


def solution(mesh):
    fine = Mesh(mesh.devices.reshape(tuple(AXES.values())), tuple(AXES))
    group, shard = ("zl", "x", "c"), ("zh", "ya", "yb", "yc")
    placed = (
        P(shard, group, None, None),
        P(shard, group, None, None),
        P(shard, None),
        P(group, shard, None, None),
        P(),
        P(),
    )
    return jax.shard_map(
        shards,
        mesh=fine,
        in_specs=placed,
        out_specs=(P(shard, None), P(group, shard, None, None)),
        check_vma=False,
    )
```

time: 85.2 us -> 77.2 us (0.906)
  blocking collectives: 68 us -> 37.1 us
  starting transfers between devices: 5.44 us -> 24.7 us
  waiting for transfers between devices: 0.46 us -> 3.92 us
    all_to_all x4 -> x2, blocking collectives: 68 us -> 37.1 us  [exchange(): return lax.all_to_all(x, axes, split_axis=0, concat_axis=0, tiled=True)]
    ppermute x0 -> x3, starting transfers between devices: none -> 16.8 us  [the longest x1 8.81 us: shards(): got = lax.ppermute(give, 'c', [(0, 1), (1, 0)])]
    ppermute x0 -> x3, waiting for transfers between devices: none -> 3.46 us  [the longest x1 2.53 us: shards(): second = lax.ppermute(second, tuple(AXES), routes(1))]
    ppermute x1, starting transfers between devices: 5.44 us -> 7.91 us  [shards(): other = lax.ppermute(mine, 'c', [(0, 1), (1, 0)])]
    unnamed x11 -> x14, local copies, waits for them, and re-layouts: 2.81 us -> 3.37 us
  transfers between devices with their start and end apart: 1 -> 4, of which waited for: 1 -> 3; matrix products, arithmetic and copies ran while one was open for 2% -> 2% of each run, Pallas kernels for 0% -> 0%
where the time goes in v2:
time: 77.2 us; the launch traced here: 76.6 us
  blocking collectives  37.1 us (48%)
  starting transfers between devices  24.7 us (32%)
  Pallas kernels  5.44 us (7%)
  waiting for transfers between devices  3.92 us (5%)
  local copies, waits for them, and re-layouts  3.37 us (4%)
  matrix products  1.41 us (2%)
    all_to_all x2, blocking collectives, exchange(): return lax.all_to_all(x, axes, split_axis=0, concat_axis=0, tiled=True)  37.1 us
    ppermute x1, starting transfers between devices, shards(): got = lax.ppermute(give, 'c', [(0, 1), (1, 0)])  8.81 us
    ppermute x1, starting transfers between devices, shards(): other = lax.ppermute(mine, 'c', [(0, 1), (1, 0)])  7.91 us
    pallas_call x5, Pallas kernels, call(): pl.pallas_call(kernel, out_shape=outs, in_specs=specs, out_specs=(VMEM,)...  5.44 us
    ppermute x1, starting transfers between devices, shards(): second = lax.ppermute(second, tuple(AXES), routes(1))  4.29 us
    ppermute x1, starting transfers between devices, shards(): first = lax.ppermute(first, tuple(AXES), routes(0))  3.66 us
    unnamed x14, local copies, waits for them, and re-layouts  3.37 us
    ppermute x1, waiting for transfers between devices, shards(): second = lax.ppermute(second, tuple(AXES), routes(1))  2.53 us
  transfers between devices with their start and end apart: 4, of which 3 were waited for; matrix products, arithmetic and copies ran while one was open for 2% of the time, Pallas kernels for 0%

profile of v2, /device:TPU:1, one launch (start us, length us, event | category | flops | bytes accessed | tf_op | source)
XLA Modules:
  0.0 76.6 jit_solution(8617560414344024885)
XLA Ops:
  0.6 0.0 copy-start
  0.6 0.0 copy-start.2
  0.7 1.1 %copy-done.2 = f32[1,6,128,128]{3,2,1,0:T(8,128)S(1)} copy-done((f32[1,6,128,128]{3,2,1,0:T(8,128)S(1)}, f32[1,6,128,128]{3,2,1,0:T(8,128)}, u32[]{:S(2)}) %copy-start.2) | copy-done | bytes 393240
  1.7 0.9 %copy-done.3 = bf16[1,6,128,128]{3,2,1,0:T(8,128)(2,1)S(1)} copy-done((bf16[1,6,128,128]{3,2,1,0:T(8,128)(2,1)S(1)}, bf16[1,6,128,128]{3,2,1,0:T(8,128)(2,1)}, u32[]{:S(2)}) %copy-start.3) | copy-done | bytes 196632
  2.7 0.7 copy-done.4
  3.4 1.6 %encode.1 = (bf16[3,128,128]{2,1,0:T(8,128)(2,1)S(1)}, bf16[3,128,128]{2,1,0:T(8,128)(2,1)S(1)}) custom-call(s32[16,32]{1,0:T(8,128)S(1)} %bitcast.7, f32[1,6,128,128]{3,2,1,0:T(8,128)S(1)} %copy-done.2, bf16[1,6,128,128]{3,2,1,0:T(8,128)(2,1)S(1)} %copy-done.3), custom_call_target="tpu_custom_call" | custom-call | tf_op jit(solution)/shard_map/encode/pallas_call | solution.py:126
  5.0 8.8 %collective-permute-start = (bf16[3,128,128]{2,1,0:T(8,128)(2,1)S(1)}, bf16[3,128,128]{2,1,0:T(8,128)(2,1)S(1)}, u32[]{:S(2)}, u32[]{:S(2)}) collective-permute-start(bf16[3,128,128]{2,1,0:T(8,128)(2,1)S(1)} %get-tuple-element.7), channel_id=1, source_target_pairs={{0,32},{32,0},{1,33},{33,1},{2,34},{34,2},{3,35},{35,3},{4,36},{36... | collective-permute-start | bytes 294920 | tf_op jit(solution)/shard_map/ppermute | solution.py:156
  13.8 0.9 %collective-permute-done.got = bf16[3,128,128]{2,1,0:T(8,128)(2,1)S(1)} collective-permute-done((bf16[3,128,128]{2,1,0:T(8,128)(2,1)S(1)}, bf16[3,128,128]{2,1,0:T(8,128)(2,1)S(1)}, u32[]{:S(2)}, u32[]{:S(2)}) %collective-permute-start) | collective-permute-done | bytes 98336 | tf_op jit(solution)/shard_map/ppermute | solution.py:156
  14.8 0.7 copy-done.5
  15.4 1.0 %home.1 = bf16[16,3,64,128]{3,2,1,0:T(8,128)(2,1)S(1)} custom-call(s32[16,32]{1,0:T(8,128)S(1)} %bitcast.8, s32[8]{0:T(128)S(1)} %copy-done.5, bf16[3,128,128]{2,1,0:T(8,128)(2,1)S(1)} %get-tuple-element.6.keep, bf16[3,128,128]{2,1,0:T(8,128)(2,1)S(1)} %collective-permute-done.got), custom_call_target="tpu_custom_call" | custom-call | tf_op jit(solution)/shard_map/home/pallas_call | solution.py:126
  16.4 14.7 %all_to_all.10.got = bf16[16,3,64,128]{3,2,1,0:T(8,128)(2,1)S(1)} all-to-all(bf16[16,3,64,128]{3,2,1,0:T(8,128)(2,1)S(1)} %home.1), channel_id=1, replica_groups=mesh['zl'=2,'x'=4,'c'=2,'zh'=4,'ya'=2,'yb'=2,'yc'=2] {'zl','x','yc'}, dimensions={0} | all-to-all | bytes 1572864 | tf_op jit(solution)/shard_map/all_to_all | solution.py:137
  31.1 0.0 copy-done.6
  31.1 0.9 %part.1 = (bf16[3,64,128]{2,1,0:T(8,128)(2,1)S(1)}, bf16[3,64,128]{2,1,0:T(8,128)(2,1)S(1)}) custom-call(s32[16,32]{1,0:T(8,128)S(1)} %bitcast.9, s32[8]{0:T(128)S(1)} %copy-done.6, bf16[16,3,64,128]{3,2,1,0:T(8,128)(2,1)S(1)} %all_to_all.10.got), custom_call_target="tpu_custom_call" | custom-call | tf_op jit(solution)/shard_map/part/pallas_call | solution.py:126
  32.0 3.7 %collective-permute-start.1 = (bf16[3,64,128]{2,1,0:T(8,128)(2,1)S(1)}, bf16[3,64,128]{2,1,0:T(8,128)(2,1)S(1)}, u32[]{:S(2)}, u32[]{:S(2)}) collective-permute-start(bf16[3,64,128]{2,1,0:T(8,128)(2,1)S(1)} %get-tuple-element.8), channel_id=1, source_target_pairs={{0,0},{1,4},{2,1},{3,5},{4,2},{5,6},{6,3},{7,7},{8,8},{9,12},{10,9... | collective-permute-start | bytes 147464 | tf_op jit(solution)/shard_map/ppermute | solution.py:164
  35.7 4.3 %collective-permute-start.2 = (bf16[3,64,128]{2,1,0:T(8,128)(2,1)S(1)}, bf16[3,64,128]{2,1,0:T(8,128)(2,1)S(1)}, u32[]{:S(2)}, u32[]{:S(2)}) collective-permute-start(bf16[3,64,128]{2,1,0:T(8,128)(2,1)S(1)} %get-tuple-element.9), channel_id=1, source_target_pairs={{0,4},{1,0},{2,5},{3,1},{4,6},{5,2},{6,7},{7,3},{8,12},{9,8},{10,1... | collective-permute-start | bytes 147464 | tf_op jit(solution)/shard_map/ppermute | solution.py:165
  40.0 0.0 collective-permute-done.1.first
  40.0 2.5 %collective-permute-done.2.second = bf16[3,64,128]{2,1,0:T(8,128)(2,1)S(1)} collective-permute-done((bf16[3,64,128]{2,1,0:T(8,128)(2,1)S(1)}, bf16[3,64,128]{2,1,0:T(8,128)(2,1)S(1)}, u32[]{:S(2)}, u32[]{:S(2)}) %collective-permute-start.2) | collective-permute-done | bytes 49184 | tf_op jit(solution)/shard_map/ppermute | solution.py:165
  42.5 0.1 spread.1
  42.6 22.4 %all_to_all.11.mine = bf16[8,3,128,128]{3,2,1,0:T(8,128)(2,1)S(1)} all-to-all(bf16[8,3,128,128]{3,2,1,0:T(8,128)(2,1)S(1)} %spread.1), channel_id=1, replica_groups=mesh['zl'=2,'x'=4,'c'=2,'zh'=4,'ya'=2,'yb'=2,'yc'=2] {'zl','x'}, dimensions={0} | all-to-all | bytes 1572864 | tf_op jit(solution)/shard_map/all_to_all | solution.py:137
  65.0 7.9 %collective-permute-start.3 = (bf16[8,3,128,128]{3,2,1,0:T(8,128)(2,1)S(1)}, bf16[8,3,128,128]{3,2,1,0:T(8,128)(2,1)S(1)}, u32[]{:S(2)}, u32[]{:S(2)}) collective-permute-start(bf16[8,3,128,128]{3,2,1,0:T(8,128)(2,1)S(1)} %all_to_all.11.mine), channel_id=1, source_target_pairs={{0,32},{32,0},{1,33},{33,1},{2,34},{34,2},{3,35},{35,3},{4,36},{36... | collective-permute-start | bytes 2359304 | tf_op jit(solution)/shard_map/ppermute | solution.py:168
  72.9 0.0 copy-done
  73.0 1.4 %fusion = bf16[1,1,256,384]{3,2,1,0:T(8,128)(2,1)} fusion(bf16[384,2048]{1,0:T(8,128)(2,1)S(1)} %copy-done.1, bf16[1,1,256,2048]{3,2,1,0:T(8,128)(2,1)S(1)} %copy-done), kind=kOutput, calls=%fused_computation.1 | convolution fusion | flops 402751488 | bytes 2818048 | tf_op jit(solution)/shard_map/dot_general | solution.py:169
  74.4 0.5 collective-permute-done.3.other
  74.8 1.8 %add.1 = bf16[384,2048]{1,0:T(8,128)(2,1)} custom-call(bf16[8,3,128,128]{3,2,1,0:T(8,128)(2,1)S(1)} %all_to_all.11.mine, bf16[8,3,128,128]{3,2,1,0:T(8,128)(2,1)S(1)} %collective-permute-done.3.other, bf16[384,2048]{1,0:T(8,128)(2,1)S(1)} %copy-done.1), custom_call_target="tpu_custom_call" | custom-call | tf_op jit(solution)/shard_map/add/pallas_call | solution.py:126
  (6 shorter events, 0.0 us)
Async XLA Ops:
  0.6 72.3 %copy-start = (bf16[1,1,256,2048]{3,2,1,0:T(8,128)(2,1)S(1)}, bf16[1,1,256,2048]{3,2,1,0:T(8,128)(2,1)}, u32[]{:S(2)}) copy-start(bf16[1,1,256,2048]{3,2,1,0:T(8,128)(2,1)} %param.9) | copy-start | bytes 3145732
  0.6 1.1 %copy-start.2 = (f32[1,6,128,128]{3,2,1,0:T(8,128)S(1)}, f32[1,6,128,128]{3,2,1,0:T(8,128)}, u32[]{:S(2)}) copy-start(f32[1,6,128,128]{3,2,1,0:T(8,128)} %master.1) | copy-start | bytes 1179652
  1.7 0.9 %copy-start.3 = (bf16[1,6,128,128]{3,2,1,0:T(8,128)(2,1)S(1)}, bf16[1,6,128,128]{3,2,1,0:T(8,128)(2,1)}, u32[]{:S(2)}) copy-start(bf16[1,6,128,128]{3,2,1,0:T(8,128)(2,1)} %sent.1) | copy-start | bytes 589828
  2.7 0.7 copy-start.4
  3.4 27.8 %copy-start.6 = (s32[8]{0:T(128)S(1)}, s32[8]{0:T(128)}, u32[]{:S(2)}) copy-start(s32[8]{0:T(128)} %slots.3) | copy-start | bytes 100
  5.0 9.7 %collective-permute-start = (bf16[3,128,128]{2,1,0:T(8,128)(2,1)S(1)}, bf16[3,128,128]{2,1,0:T(8,128)(2,1)S(1)}, u32[]{:S(2)}, u32[]{:S(2)}) collective-permute-start(bf16[3,128,128]{2,1,0:T(8,128)(2,1)S(1)} %get-tuple-element.7), channel_id=1, source_target_pairs={{0,32},{32,0},{1,33},{33,1},{2,34},{34,2},{3,35},{35,3},{4,36},{36... | collective-permute-start | bytes 294920 | tf_op jit(solution)/shard_map/ppermute | solution.py:156
  14.7 0.7 copy-start.5
  31.1 41.8 %copy-start.1 = (bf16[384,2048]{1,0:T(8,128)(2,1)S(1)}, bf16[384,2048]{1,0:T(8,128)(2,1)}, u32[]{:S(2)}) copy-start(bf16[384,2048]{1,0:T(8,128)(2,1)} %base.1) | copy-start | bytes 4718596
  32.0 8.0 %collective-permute-start.1 = (bf16[3,64,128]{2,1,0:T(8,128)(2,1)S(1)}, bf16[3,64,128]{2,1,0:T(8,128)(2,1)S(1)}, u32[]{:S(2)}, u32[]{:S(2)}) collective-permute-start(bf16[3,64,128]{2,1,0:T(8,128)(2,1)S(1)} %get-tuple-element.8), channel_id=1, source_target_pairs={{0,0},{1,4},{2,1},{3,5},{4,2},{5,6},{6,3},{7,7},{8,8},{9,12},{10,9... | collective-permute-start | bytes 147464 | tf_op jit(solution)/shard_map/ppermute | solution.py:164
  35.7 6.8 %collective-permute-start.2 = (bf16[3,64,128]{2,1,0:T(8,128)(2,1)S(1)}, bf16[3,64,128]{2,1,0:T(8,128)(2,1)S(1)}, u32[]{:S(2)}, u32[]{:S(2)}) collective-permute-start(bf16[3,64,128]{2,1,0:T(8,128)(2,1)S(1)} %get-tuple-element.9), channel_id=1, source_target_pairs={{0,4},{1,0},{2,5},{3,1},{4,6},{5,2},{6,7},{7,3},{8,12},{9,8},{10,1... | collective-permute-start | bytes 147464 | tf_op jit(solution)/shard_map/ppermute | solution.py:165
  65.0 9.8 %collective-permute-start.3 = (bf16[8,3,128,128]{3,2,1,0:T(8,128)(2,1)S(1)}, bf16[8,3,128,128]{3,2,1,0:T(8,128)(2,1)S(1)}, u32[]{:S(2)}, u32[]{:S(2)}) collective-permute-start(bf16[8,3,128,128]{3,2,1,0:T(8,128)(2,1)S(1)} %all_to_all.11.mine), channel_id=1, source_target_pairs={{0,32},{32,0},{1,33},{33,1},{2,34},{34,2},{3,35},{35,3},{4,36},{36... | collective-permute-start | bytes 2359304 | tf_op jit(solution)/shard_map/ppermute | solution.py:168

commit v3 on v2

v3 whole, which is shorter than its diff:
```python
import jax
import jax.numpy as jnp
from jax import lax
from jax.experimental import pallas as pl
from jax.experimental.pallas import tpu as pltpu
from jax.sharding import Mesh
from jax.sharding import PartitionSpec as P

CLIP_RATIO = 2.5
EPSILON = 1e-06

AXES = {"zl": 2, "x": 4, "c": 2, "zh": 4, "ya": 2, "yb": 2, "yc": 2}
BLK = 128
HALF = 64
PART = 16
TROWS = 12
MOST = 6
GROUPS = 16
EXPERTS = 8


class Place:
    def __init__(self):
        at = {name: lax.axis_index(name) for name in AXES}
        self.c, self.x, self.yb, self.yc = at["c"], at["x"], at["yb"], at["yc"]
        self.g = at["zl"] * 8 + at["x"] * 2 + at["c"]
        self.col = at["zh"] * 4 + at["ya"] * 2 + at["yb"]
        self.s = 2 * self.col + at["yc"]


def run_of(lengths, s, g):
    start = jnp.int32(0)
    for i in range(GROUPS):
        start += jnp.where(i < g, lengths[i, s], 0)
    return start, lengths[g, s]


def encode_kernel(master, sent, keep, give):
    at = Place()
    change = master[0, 0] - sent[0, 0].astype(jnp.float32)
    mean = jnp.sum(change * change, axis=(0, 1), keepdims=True) * (1.0 / (BLK * BLK))
    scale = jnp.sqrt(mean + EPSILON).astype(jnp.bfloat16).astype(jnp.float32)
    encoded = jnp.clip(change / scale, -CLIP_RATIO, CLIP_RATIO).astype(jnp.bfloat16)
    value = (encoded.astype(jnp.float32) * scale).astype(jnp.bfloat16)
    low = at.c == 0
    keep[0] = jnp.where(low, value[:HALF], value[HALF:])
    give[0] = jnp.where(low, value[HALF:], value[:HALF])


def home_kernel(lengths, keep, got, out):
    at = Place()
    for tiles, g in ((keep, at.g), (got, at.g ^ 1)):
        start, count = run_of(lengths, at.s, g)
        for j in range(MOST):
            r = lax.rem(start + j, TROWS)
            k, i = lax.div(r, 3), lax.rem(r, 3)
            to = ((k >> 1) ^ at.yb) * 2 + (k & 1)

            @pl.when(j < count)
            def _():
                for n in range(4):
                    out[to + 4 * n, i] = tiles[j, n * PART : (n + 1) * PART, :]


def slot_kernel(lengths, slots, got, out):
    at = Place()
    kb = (at.x & 1) ^ at.yb
    first = 3 * (2 * kb + at.yc)
    ends = []
    for side in range(2):
        end, row = jnp.int32(0), []
        for n in range(GROUPS - 1):
            end += lengths[n, 2 * at.col + side]
            row.append(end)
        ends.append(row)
    for e in range(EXPERTS):
        to = 2 * slots[e] + kb
        for i in range(3):
            q = (e % 4) * TROWS + first + i
            owner = jnp.int32(0)
            for end in ends[e // 4]:
                owner += jnp.where(end <= q, 1, 0)
            out[to, i] = got[(owner & 14) + e // 4, i]


def spread_kernel(got, out):
    at = Place()
    side = (at.x & 1) ^ at.yb
    for n in range(8):
        for i in range(3):
            part = got[2 * n + side, i]
            for to in range(8):
                out[to, n, i] = part


def add_kernel(mine, other, base, out):
    at = Place()
    near = at.c == 0
    for col in range(16):
        cols = pl.ds(col * BLK, BLK)
        side = (col & 1) ^ at.yb
        for n in range(4):
            chip = 2 * n + side
            for i in range(3):
                a, b = mine[chip, col >> 1, i], other[chip, col >> 1, i]
                for half in range(2):
                    part = (jnp.where(near, b, a) if half else jnp.where(near, a, b)).astype(jnp.float32)
                    rows = pl.ds(i * BLK + half * HALF + n * PART, PART)
                    out[rows, cols] = (base[rows, cols].astype(jnp.float32) + part).astype(jnp.bfloat16)


SMEM = pl.BlockSpec(memory_space=pltpu.SMEM)
VMEM = pl.BlockSpec(memory_space=pltpu.VMEM)
LIMIT = pltpu.CompilerParams(vmem_limit_bytes=32 * 1024 * 1024)


def call(kernel, name, specs, shapes, *args):
    outs = tuple(jax.ShapeDtypeStruct(s, jnp.bfloat16) for s in shapes)
    return pl.pallas_call(
        kernel,
        out_shape=outs,
        in_specs=specs,
        out_specs=(VMEM,) * len(outs),
        compiler_params=LIMIT,
        name=name,
    )(*args)


def exchange(x, axes):
    return lax.all_to_all(x, axes, split_axis=0, concat_axis=0, tiled=True)


def shards(master_new, sent_base, rollout_base, tokens, lengths, expert_slot):
    lengths = lengths.T
    halves = jax.ShapeDtypeStruct((MOST, HALF, BLK), jnp.bfloat16)
    keep, give = pl.pallas_call(
        encode_kernel,
        grid=(MOST,),
        out_shape=(halves, halves),
        in_specs=[pl.BlockSpec((1, 1, BLK, BLK), lambda j: (0, j, 0, 0))] * 2,
        out_specs=(pl.BlockSpec((1, HALF, BLK), lambda j: (j, 0, 0)),) * 2,
        compiler_params=LIMIT,
        name="encode",
    )(master_new, sent_base)
    got = lax.ppermute(give, "c", [(0, 1), (1, 0)])
    (out,) = call(home_kernel, "home", [SMEM, VMEM, VMEM], [(16, 3, PART, BLK)], lengths, keep, got)
    out = exchange(out, ("zl", "x", "yc"))
    (out,) = call(slot_kernel, "slot", [SMEM, SMEM, VMEM], [(16, 3, PART, BLK)], lengths, expert_slot, out)
    out = exchange(out, ("zh", "ya", "yb"))
    (out,) = call(spread_kernel, "spread", [VMEM], [(8, 8, 3, PART, BLK)], out)
    mine = exchange(out, ("zl", "x"))
    other = lax.ppermute(mine, "c", [(0, 1), (1, 0)])
    in_flight = lax.dot_general(
        tokens[0, 0], rollout_base, (((1,), (1,)), ((), ())), preferred_element_type=jnp.float32
    ).astype(jnp.bfloat16)[None, None]
    (new_weights,) = call(
        add_kernel, "add", [VMEM, VMEM, VMEM], [rollout_base.shape], mine, other, rollout_base
    )
    return (new_weights, in_flight)


def solution(mesh):
    fine = Mesh(mesh.devices.reshape(tuple(AXES.values())), tuple(AXES))
    group, shard = ("zl", "x", "c"), ("zh", "ya", "yb", "yc")
    placed = (
        P(shard, group, None, None),
        P(shard, group, None, None),
        P(shard, None),
        P(group, shard, None, None),
        P(),
        P(),
    )
    return jax.shard_map(
        shards,
        mesh=fine,
        in_specs=placed,
        out_specs=(P(shard, None), P(group, shard, None, None)),
        check_vma=False,
    )
```

time: 77.2 us -> 73 us (0.946)
  starting transfers between devices: 24.7 us -> 15.5 us
  blocking collectives: 37.1 us -> 44.5 us
  waiting for transfers between devices: 3.92 us -> 1.38 us
    ppermute x2 -> x0, starting transfers between devices: 7.95 us -> none  [the longest x1 4.29 us: shards(): second = lax.ppermute(second, tuple(AXES), routes(1))]
    all_to_all x2 -> x3, blocking collectives: 37.1 us -> 44.5 us  [exchange(): return lax.all_to_all(x, axes, split_axis=0, concat_axis=0, tiled=True)]
    ppermute x2 -> x0, waiting for transfers between devices: 2.53 us -> none  [the longest x1 2.53 us: shards(): second = lax.ppermute(second, tuple(AXES), routes(1))]
    pallas_call x5 -> x4, Pallas kernels: 5.44 us -> 4.06 us  [call(): pl.pallas_call(kernel, out_shape=outs, in_specs=specs, out_specs=(VMEM,)...]
    ppermute x1, starting transfers between devices: 7.91 us -> 6.67 us  [shards(): other = lax.ppermute(mine, 'c', [(0, 1), (1, 0)])]
    pallas_call x0 -> x1, Pallas kernels: none -> 1.07 us  [shards(): pl.pallas_call(encode_kernel, grid=(MOST,), out_shape=(halves, halves), i...]
  transfers between devices with their start and end apart: 4 -> 2, of which waited for: 3 -> 2; matrix products, arithmetic and copies ran while one was open for 2% -> 2% of each run, Pallas kernels for 0% -> 0%
where the time goes in v3:
time: 73 us; the launch traced here: 72.6 us
  blocking collectives  44.5 us (61%)
  starting transfers between devices  15.5 us (21%)
  Pallas kernels  5.13 us (7%)
  local copies, waits for them, and re-layouts  4.07 us (6%)
  matrix products  1.41 us (2%)
  waiting for transfers between devices  1.38 us (2%)
    all_to_all x3, blocking collectives, exchange(): return lax.all_to_all(x, axes, split_axis=0, concat_axis=0, tiled=True)  44.5 us
    ppermute x1, starting transfers between devices, shards(): got = lax.ppermute(give, 'c', [(0, 1), (1, 0)])  8.79 us
    ppermute x1, starting transfers between devices, shards(): other = lax.ppermute(mine, 'c', [(0, 1), (1, 0)])  6.67 us
    unnamed x14, local copies, waits for them, and re-layouts  4.07 us
    pallas_call x4, Pallas kernels, call(): pl.pallas_call(kernel, out_shape=outs, in_specs=specs, out_specs=(VMEM,)...  4.06 us
  transfers between devices with their start and end apart: 2, of which 2 were waited for; matrix products, arithmetic and copies ran while one was open for 2% of the time, Pallas kernels for 0%

profile of v3, /device:TPU:1, one launch (start us, length us, event | category | flops | bytes accessed | tf_op | source)
XLA Modules:
  0.0 72.6 jit_solution(17371522469514480183)
XLA Ops:
  0.6 0.0 copy-start
  0.6 0.0 copy-start.2
  0.7 1.1 %copy-done.2 = f32[1,6,128,128]{3,2,1,0:T(8,128)S(1)} copy-done((f32[1,6,128,128]{3,2,1,0:T(8,128)S(1)}, f32[1,6,128,128]{3,2,1,0:T(8,128)}, u32[]{:S(2)}) %copy-start.2) | copy-done | bytes 393240
  1.7 0.0 copy-start.3
  1.7 0.9 %copy-done.3 = bf16[1,6,128,128]{3,2,1,0:T(8,128)(2,1)S(1)} copy-done((bf16[1,6,128,128]{3,2,1,0:T(8,128)(2,1)S(1)}, bf16[1,6,128,128]{3,2,1,0:T(8,128)(2,1)}, u32[]{:S(2)}) %copy-start.3) | copy-done | bytes 196632
  2.7 1.1 %encode.1 = (bf16[6,64,128]{2,1,0:T(8,128)(2,1)S(1)}, bf16[6,64,128]{2,1,0:T(8,128)(2,1)S(1)}) custom-call(f32[1,6,128,128]{3,2,1,0:T(8,128)S(1)} %copy-done.2, bf16[1,6,128,128]{3,2,1,0:T(8,128)(2,1)S(1)} %copy-done.3), custom_call_target="tpu_custom_call" | custom-call | tf_op jit(solution)/shard_map/encode/pallas_call | solution.py:136
  3.7 8.8 %collective-permute-start = (bf16[6,64,128]{2,1,0:T(8,128)(2,1)S(1)}, bf16[6,64,128]{2,1,0:T(8,128)(2,1)S(1)}, u32[]{:S(2)}, u32[]{:S(2)}) collective-permute-start(bf16[6,64,128]{2,1,0:T(8,128)(2,1)S(1)} %get-tuple-element.5), channel_id=1, source_target_pairs={{0,32},{32,0},{1,33},{33,1},{2,34},{34,2},{3,35},{35,3},{4,36},{36... | collective-permute-start | bytes 294920 | tf_op jit(solution)/shard_map/ppermute | solution.py:145
  12.5 0.9 %collective-permute-done.got = bf16[6,64,128]{2,1,0:T(8,128)(2,1)S(1)} collective-permute-done((bf16[6,64,128]{2,1,0:T(8,128)(2,1)S(1)}, bf16[6,64,128]{2,1,0:T(8,128)(2,1)S(1)}, u32[]{:S(2)}, u32[]{:S(2)}) %collective-permute-start) | collective-permute-done | bytes 98336 | tf_op jit(solution)/shard_map/ppermute | solution.py:145
  13.5 0.7 copy-done.4
  14.1 1.0 %home.1 = bf16[16,3,16,128]{3,2,1,0:T(8,128)(2,1)S(1)} custom-call(s32[16,32]{1,0:T(8,128)S(1)} %bitcast.7, bf16[6,64,128]{2,1,0:T(8,128)(2,1)S(1)} %get-tuple-element.4.keep, bf16[6,64,128]{2,1,0:T(8,128)(2,1)S(1)} %collective-permute-done.got), custom_call_target="tpu_custom_call" | custom-call | tf_op jit(solution)/shard_map/home/pallas_call | solution.py:119
  15.1 8.8 %all_to_all.15.got = bf16[16,3,16,128]{3,2,1,0:T(8,128)(2,1)S(1)} all-to-all(bf16[16,3,16,128]{3,2,1,0:T(8,128)(2,1)S(1)} %home.1), channel_id=1, replica_groups=mesh['zl'=2,'x'=4,'c'=2,'zh'=4,'ya'=2,'yb'=2,'yc'=2] {'zl','x','yc'}, dimensions={0} | all-to-all | bytes 393216 | tf_op jit(solution)/shard_map/all_to_all | solution.py:130
  23.9 0.7 copy-done.5
  24.6 0.7 copy-done.6
  25.2 1.2 %slot.1 = bf16[16,3,16,128]{3,2,1,0:T(8,128)(2,1)S(1)} custom-call(s32[16,32]{1,0:T(8,128)S(1)} %bitcast.8, s32[8]{0:T(128)S(1)} %copy-done.6, bf16[16,3,16,128]{3,2,1,0:T(8,128)(2,1)S(1)} %all_to_all.15.got), custom_call_target="tpu_custom_call" | custom-call | tf_op jit(solution)/shard_map/slot/pallas_call | solution.py:119
  26.5 0.0 copy-start.1
  26.5 23.8 %all_to_all.16.got = bf16[16,3,16,128]{3,2,1,0:T(8,128)(2,1)S(1)} all-to-all(bf16[16,3,16,128]{3,2,1,0:T(8,128)(2,1)S(1)} %slot.1), channel_id=1, replica_groups=mesh['zl'=2,'x'=4,'c'=2,'zh'=4,'ya'=2,'yb'=2,'yc'=2] {'zh','ya','yb'}, dimensions={0} | all-to-all | bytes 393216 | tf_op jit(solution)/shard_map/all_to_all | solution.py:130
  50.3 0.1 spread.1
  50.4 11.8 %all_to_all.17.mine = bf16[8,8,3,16,128]{4,3,2,1,0:T(8,128)(2,1)S(1)} all-to-all(bf16[8,8,3,16,128]{4,3,2,1,0:T(8,128)(2,1)S(1)} %spread.1), channel_id=1, replica_groups=mesh['zl'=2,'x'=4,'c'=2,'zh'=4,'ya'=2,'yb'=2,'yc'=2] {'zl','x'}, dimensions={0} | all-to-all | bytes 1572864 | tf_op jit(solution)/shard_map/all_to_all | solution.py:130
  62.3 6.7 %collective-permute-start.1 = (bf16[8,8,3,16,128]{4,3,2,1,0:T(8,128)(2,1)S(1)}, bf16[8,8,3,16,128]{4,3,2,1,0:T(8,128)(2,1)S(1)}, u32[]{:S(2)}, u32[]{:S(2)}) collective-permute-start(bf16[8,8,3,16,128]{4,3,2,1,0:T(8,128)(2,1)S(1)} %all_to_all.17.mine), channel_id=1, source_target_pairs={{0,32},{32,0},{1,33},{33,1},{2,34},{34,2},{3,35},{35,3},{4,36},{36... | collective-permute-start | bytes 2359304 | tf_op jit(solution)/shard_map/ppermute | solution.py:152
  68.9 0.0 copy-done
  69.0 0.0 copy-done.1
  69.0 1.4 %fusion = bf16[1,1,256,384]{3,2,1,0:T(8,128)(2,1)} fusion(bf16[384,2048]{1,0:T(8,128)(2,1)S(1)} %copy-done.1, bf16[1,1,256,2048]{3,2,1,0:T(8,128)(2,1)S(1)} %copy-done), kind=kOutput, calls=%fused_computation.1 | convolution fusion | flops 402751488 | bytes 2818048 | tf_op jit(solution)/shard_map/dot_general | solution.py:153
  70.4 0.5 collective-permute-done.1.other
  70.8 1.8 %add.1 = bf16[384,2048]{1,0:T(8,128)(2,1)} custom-call(bf16[8,8,3,16,128]{4,3,2,1,0:T(8,128)(2,1)S(1)} %all_to_all.17.mine, bf16[8,8,3,16,128]{4,3,2,1,0:T(8,128)(2,1)S(1)} %collective-permute-done.1.other, bf16[384,2048]{1,0:T(8,128)(2,1)S(1)} %copy-done.1), custom_call_target="tpu_custom_call" | custom-call | tf_op jit(solution)/shard_map/add/pallas_call | solution.py:119
  (3 shorter events, 0.0 us)
Async XLA Ops:
  0.6 68.3 %copy-start = (bf16[1,1,256,2048]{3,2,1,0:T(8,128)(2,1)S(1)}, bf16[1,1,256,2048]{3,2,1,0:T(8,128)(2,1)}, u32[]{:S(2)}) copy-start(bf16[1,1,256,2048]{3,2,1,0:T(8,128)(2,1)} %param.9) | copy-start | bytes 3145732
  0.6 1.1 %copy-start.2 = (f32[1,6,128,128]{3,2,1,0:T(8,128)S(1)}, f32[1,6,128,128]{3,2,1,0:T(8,128)}, u32[]{:S(2)}) copy-start(f32[1,6,128,128]{3,2,1,0:T(8,128)} %master.1) | copy-start | bytes 1179652
  1.7 0.9 %copy-start.3 = (bf16[1,6,128,128]{3,2,1,0:T(8,128)(2,1)S(1)}, bf16[1,6,128,128]{3,2,1,0:T(8,128)(2,1)}, u32[]{:S(2)}) copy-start(bf16[1,6,128,128]{3,2,1,0:T(8,128)(2,1)} %sent.1) | copy-start | bytes 589828
  3.7 9.7 %collective-permute-start = (bf16[6,64,128]{2,1,0:T(8,128)(2,1)S(1)}, bf16[6,64,128]{2,1,0:T(8,128)(2,1)S(1)}, u32[]{:S(2)}, u32[]{:S(2)}) collective-permute-start(bf16[6,64,128]{2,1,0:T(8,128)(2,1)S(1)} %get-tuple-element.5), channel_id=1, source_target_pairs={{0,32},{32,0},{1,33},{33,1},{2,34},{34,2},{3,35},{35,3},{4,36},{36... | collective-permute-start | bytes 294920 | tf_op jit(solution)/shard_map/ppermute | solution.py:145
  13.5 0.7 copy-start.4
  23.9 0.7 copy-start.5
  24.6 0.7 copy-start.6
  26.5 42.5 %copy-start.1 = (bf16[384,2048]{1,0:T(8,128)(2,1)S(1)}, bf16[384,2048]{1,0:T(8,128)(2,1)}, u32[]{:S(2)}) copy-start(bf16[384,2048]{1,0:T(8,128)(2,1)} %base.1) | copy-start | bytes 4718596
  62.3 8.6 %collective-permute-start.1 = (bf16[8,8,3,16,128]{4,3,2,1,0:T(8,128)(2,1)S(1)}, bf16[8,8,3,16,128]{4,3,2,1,0:T(8,128)(2,1)S(1)}, u32[]{:S(2)}, u32[]{:S(2)}) collective-permute-start(bf16[8,8,3,16,128]{4,3,2,1,0:T(8,128)(2,1)S(1)} %all_to_all.17.mine), channel_id=1, source_target_pairs={{0,32},{32,0},{1,33},{33,1},{2,34},{34,2},{3,35},{35,3},{4,36},{36... | collective-permute-start | bytes 2359304 | tf_op jit(solution)/shard_map/ppermute | solution.py:152

commit v4 on v3

--- a/solution.py
+++ b/solution.py
@@ -35,31 +35,40 @@
     return start, lengths[g, s]
 
 
-def encode_kernel(master, sent, keep, give):
+def encode_kernel(lengths_in, slots_in, master_in, sent_in, out, lengths_out, slots_out, lengths, master, sent, sems):
+    loads = [
+        pltpu.make_async_copy(lengths_in, lengths, sems.at[0]),
+        pltpu.make_async_copy(lengths_in, lengths_out, sems.at[1]),
+        pltpu.make_async_copy(slots_in, slots_out, sems.at[2]),
+    ]
+    for j in range(MOST):
+        loads.append(pltpu.make_async_copy(master_in.at[0, j], master.at[j], sems.at[3 + 2 * j]))
+        loads.append(pltpu.make_async_copy(sent_in.at[0, j], sent.at[j], sems.at[4 + 2 * j]))
+    for load in loads:
+        load.start()
     at = Place()
-    change = master[0, 0] - sent[0, 0].astype(jnp.float32)
-    mean = jnp.sum(change * change, axis=(0, 1), keepdims=True) * (1.0 / (BLK * BLK))
-    scale = jnp.sqrt(mean + EPSILON).astype(jnp.bfloat16).astype(jnp.float32)
-    encoded = jnp.clip(change / scale, -CLIP_RATIO, CLIP_RATIO).astype(jnp.bfloat16)
-    value = (encoded.astype(jnp.float32) * scale).astype(jnp.bfloat16)
-    low = at.c == 0
-    keep[0] = jnp.where(low, value[:HALF], value[HALF:])
-    give[0] = jnp.where(low, value[HALF:], value[:HALF])
+    loads[0].wait()
+    start, count = run_of(lengths, at.s, at.g)
+    for j in range(MOST):
+        loads[3 + 2 * j].wait()
+        loads[4 + 2 * j].wait()
+        change = master[j] - sent[j].astype(jnp.float32)
+        mean = jnp.sum(change * change, axis=(0, 1), keepdims=True) * (1.0 / (BLK * BLK))
+        scale = jnp.sqrt(mean + EPSILON).astype(jnp.bfloat16).astype(jnp.float32)
+        encoded = jnp.clip(change / scale, -CLIP_RATIO, CLIP_RATIO).astype(jnp.bfloat16)
+        value = (encoded.astype(jnp.float32) * scale).astype(jnp.bfloat16)
+        r = lax.rem(start + j, TROWS)
+        k, i = lax.div(r, 3), lax.rem(r, 3)
+        to = ((k >> 1) ^ at.yb) * 4 + (k & 1)
 
+        @pl.when(j < count)
+        def _():
+            for n in range(8):
+                peer = (n >> 1 & 1) * 16 + (n & 1) * 8 + (n >> 2) * 2
+                out[peer + to, i] = value[n * PART : (n + 1) * PART, :]
 
-def home_kernel(lengths, keep, got, out):
-    at = Place()
-    for tiles, g in ((keep, at.g), (got, at.g ^ 1)):
-        start, count = run_of(lengths, at.s, g)
-        for j in range(MOST):
-            r = lax.rem(start + j, TROWS)
-            k, i = lax.div(r, 3), lax.rem(r, 3)
-            to = ((k >> 1) ^ at.yb) * 2 + (k & 1)
-
-            @pl.when(j < count)
-            def _():
-                for n in range(4):
-                    out[to + 4 * n, i] = tiles[j, n * PART : (n + 1) * PART, :]
+    loads[1].wait()
+    loads[2].wait()
 
 
 def slot_kernel(lengths, slots, got, out):
@@ -80,7 +89,7 @@
             owner = jnp.int32(0)
             for end in ends[e // 4]:
                 owner += jnp.where(end <= q, 1, 0)
-            out[to, i] = got[(owner & 14) + e // 4, i]
+            out[to, i] = got[2 * owner + e // 4, i]
 
 
 def spread_kernel(got, out):
@@ -111,6 +120,7 @@
 
 SMEM = pl.BlockSpec(memory_space=pltpu.SMEM)
 VMEM = pl.BlockSpec(memory_space=pltpu.VMEM)
+HBM = pl.BlockSpec(memory_space=pltpu.HBM)
 LIMIT = pltpu.CompilerParams(vmem_limit_bytes=32 * 1024 * 1024)
 
 
@@ -132,19 +142,25 @@
 
 def shards(master_new, sent_base, rollout_base, tokens, lengths, expert_slot):
     lengths = lengths.T
-    halves = jax.ShapeDtypeStruct((MOST, HALF, BLK), jnp.bfloat16)
-    keep, give = pl.pallas_call(
+    out, lengths, expert_slot = pl.pallas_call(
         encode_kernel,
-        grid=(MOST,),
-        out_shape=(halves, halves),
-        in_specs=[pl.BlockSpec((1, 1, BLK, BLK), lambda j: (0, j, 0, 0))] * 2,
-        out_specs=(pl.BlockSpec((1, HALF, BLK), lambda j: (j, 0, 0)),) * 2,
+        out_shape=(
+            jax.ShapeDtypeStruct((32, 3, PART, BLK), jnp.bfloat16),
+            jax.typeof(lengths),
+            jax.typeof(expert_slot),
+        ),
+        in_specs=[HBM] * 4,
+        out_specs=(VMEM,) * 3,
+        scratch_shapes=[
+            pltpu.SMEM(lengths.shape, jnp.int32),
+            pltpu.VMEM((MOST, BLK, BLK), jnp.float32),
+            pltpu.VMEM((MOST, BLK, BLK), jnp.bfloat16),
+            pltpu.SemaphoreType.DMA((3 + 2 * MOST,)),
+        ],
         compiler_params=LIMIT,
         name="encode",
-    )(master_new, sent_base)
-    got = lax.ppermute(give, "c", [(0, 1), (1, 0)])
-    (out,) = call(home_kernel, "home", [SMEM, VMEM, VMEM], [(16, 3, PART, BLK)], lengths, keep, got)
-    out = exchange(out, ("zl", "x", "yc"))
+    )(*(pltpu.with_memory_space_constraint(v, pltpu.HBM) for v in (lengths, expert_slot, master_new, sent_base)))
+    out = exchange(out, ("zl", "x", "c", "yc"))
     (out,) = call(slot_kernel, "slot", [SMEM, SMEM, VMEM], [(16, 3, PART, BLK)], lengths, expert_slot, out)
     out = exchange(out, ("zh", "ya", "yb"))
     (out,) = call(spread_kernel, "spread", [VMEM], [(8, 8, 3, PART, BLK)], out)

time: 73 us -> 70.2 us (0.962)
  blocking collectives: 44.5 us -> 56.5 us
  starting transfers between devices: 15.5 us -> 5.58 us
  local copies, waits for them, and re-layouts: 4.07 us -> 0.02 us
  waiting for transfers between devices: 1.38 us -> 0.46 us
    all_to_all x3, blocking collectives: 44.5 us -> 56.5 us  [exchange(): return lax.all_to_all(x, axes, split_axis=0, concat_axis=0, tiled=True)]
    ppermute x1 -> x0, starting transfers between devices: 8.79 us -> none  [shards(): got = lax.ppermute(give, 'c', [(0, 1), (1, 0)])]
    unnamed x14 -> x4, local copies, waits for them, and re-layouts: 4.07 us -> 0.02 us
    ppermute x1, starting transfers between devices: 6.67 us -> 5.58 us  [shards(): other = lax.ppermute(mine, 'c', [(0, 1), (1, 0)])]
    pallas_call x1, Pallas kernels: 1.07 us -> 2.09 us  [shards(): pl.pallas_call(encode_kernel, out_shape=(jax.ShapeDtypeStruct((32, 3, PAR...]
    pallas_call x4 -> x3, Pallas kernels: 4.06 us -> 3.12 us  [call(): pl.pallas_call(kernel, out_shape=outs, in_specs=specs, out_specs=(VMEM,)...]
    ppermute x1 -> x0, waiting for transfers between devices: 0.92 us -> none  [shards(): got = lax.ppermute(give, 'c', [(0, 1), (1, 0)])]
  transfers between devices with their start and end apart: 2 -> 1, of which waited for: 2 -> 1; matrix products, arithmetic and copies ran while one was open for 2% -> 2% of each run, Pallas kernels for 0% -> 0%
where the time goes in v4:
time: 70.2 us; the launch traced here: 69.9 us
  blocking collectives  56.5 us (80%)
  starting transfers between devices  5.58 us (8%)
  Pallas kernels  5.21 us (7%)
  matrix products  1.41 us (2%)
    all_to_all x3, blocking collectives, exchange(): return lax.all_to_all(x, axes, split_axis=0, concat_axis=0, tiled=True)  56.5 us
    ppermute x1, starting transfers between devices, shards(): other = lax.ppermute(mine, 'c', [(0, 1), (1, 0)])  5.58 us
    pallas_call x3, Pallas kernels, call(): pl.pallas_call(kernel, out_shape=outs, in_specs=specs, out_specs=(VMEM,)...  3.12 us
    pallas_call x1, Pallas kernels, shards(): pl.pallas_call(encode_kernel, out_shape=(jax.ShapeDtypeStruct((32, 3, PAR...  2.09 us
    dot_general x1, matrix products, shards(): lax.dot_general(tokens[0, 0], rollout_base, (((1,), (1,)), ((), ())), pre...  1.41 us
  transfers between devices with their start and end apart: 1, of which 1 were waited for; matrix products, arithmetic and copies ran while one was open for 2% of the time, Pallas kernels for 0%

profile of v4, /device:TPU:1, one launch (start us, length us, event | category | flops | bytes accessed | tf_op | source)
XLA Modules:
  0.0 69.9 jit_solution(17311903932053814624)
XLA Ops:
  0.6 0.0 copy-start
  0.6 2.1 %encode.1 = (bf16[32,3,16,128]{3,2,1,0:T(8,128)(2,1)S(1)}, s32[16,32]{1,0:T(8,128)S(1)}, s32[8]{0:T(128)S(1)}) custom-call(s32[16,32]{1,0:T(8,128)} %bitcast.7, s32[8]{0:T(128)} %slots_in.1, f32[1,6,128,128]{3,2,1,0:T(8,128)} %master_in.1, bf16[1,6,128,128]{3,2,1,0:T(8,128)(2,1)} %sent_in.1), custom_call_target="tpu_custom_call" | custom-call | tf_op jit(solution)/shard_map/encode/pallas_call | solution.py:145
  2.7 18.9 %all_to_all.15.got = bf16[32,3,16,128]{3,2,1,0:T(8,128)(2,1)S(1)} all-to-all(bf16[32,3,16,128]{3,2,1,0:T(8,128)(2,1)S(1)} %get-tuple-element.7), channel_id=1, replica_groups=mesh['zl'=2,'x'=4,'c'=2,'zh'=4,'ya'=2,'yb'=2,'yc'=2] {'zl','x','c','yc'}, dimensions={0} | all-to-all | bytes 786432 | tf_op jit(solution)/shard_map/all_to_all | solution.py:140
  21.6 1.2 %slot.1 = bf16[16,3,16,128]{3,2,1,0:T(8,128)(2,1)S(1)} custom-call(s32[16,32]{1,0:T(8,128)S(1)} %get-tuple-element.5.lengths, s32[8]{0:T(128)S(1)} %get-tuple-element.6.slots, bf16[32,3,16,128]{3,2,1,0:T(8,128)(2,1)S(1)} %all_to_all.15.got), custom_call_target="tpu_custom_call" | custom-call | tf_op jit(solution)/shard_map/slot/pallas_call | solution.py:129
  22.9 0.0 copy-start.1
  22.9 24.0 %all_to_all.16.got = bf16[16,3,16,128]{3,2,1,0:T(8,128)(2,1)S(1)} all-to-all(bf16[16,3,16,128]{3,2,1,0:T(8,128)(2,1)S(1)} %slot.1), channel_id=1, replica_groups=mesh['zl'=2,'x'=4,'c'=2,'zh'=4,'ya'=2,'yb'=2,'yc'=2] {'zh','ya','yb'}, dimensions={0} | all-to-all | bytes 393216 | tf_op jit(solution)/shard_map/all_to_all | solution.py:140
  46.9 0.1 spread.1
  47.0 13.6 %all_to_all.17.mine = bf16[8,8,3,16,128]{4,3,2,1,0:T(8,128)(2,1)S(1)} all-to-all(bf16[8,8,3,16,128]{4,3,2,1,0:T(8,128)(2,1)S(1)} %spread.1), channel_id=1, replica_groups=mesh['zl'=2,'x'=4,'c'=2,'zh'=4,'ya'=2,'yb'=2,'yc'=2] {'zl','x'}, dimensions={0} | all-to-all | bytes 1572864 | tf_op jit(solution)/shard_map/all_to_all | solution.py:140
  60.7 5.6 %collective-permute-start = (bf16[8,8,3,16,128]{4,3,2,1,0:T(8,128)(2,1)S(1)}, bf16[8,8,3,16,128]{4,3,2,1,0:T(8,128)(2,1)S(1)}, u32[]{:S(2)}, u32[]{:S(2)}) collective-permute-start(bf16[8,8,3,16,128]{4,3,2,1,0:T(8,128)(2,1)S(1)} %all_to_all.17.mine), channel_id=1, source_target_pairs={{0,32},{32,0},{1,33},{33,1},{2,34},{34,2},{3,35},{35,3},{4,36},{36... | collective-permute-start | bytes 2359304 | tf_op jit(solution)/shard_map/ppermute | solution.py:168
  66.2 0.0 copy-done
  66.2 0.0 copy-done.1
  66.3 1.4 %fusion = bf16[1,1,256,384]{3,2,1,0:T(8,128)(2,1)} fusion(bf16[384,2048]{1,0:T(8,128)(2,1)S(1)} %copy-done.1, bf16[1,1,256,2048]{3,2,1,0:T(8,128)(2,1)S(1)} %copy-done), kind=kOutput, calls=%fused_computation.1 | convolution fusion | flops 402751488 | bytes 2818048 | tf_op jit(solution)/shard_map/dot_general | solution.py:169
  67.7 0.5 collective-permute-done.other
  68.1 1.8 %add.1 = bf16[384,2048]{1,0:T(8,128)(2,1)} custom-call(bf16[8,8,3,16,128]{4,3,2,1,0:T(8,128)(2,1)S(1)} %all_to_all.17.mine, bf16[8,8,3,16,128]{4,3,2,1,0:T(8,128)(2,1)S(1)} %collective-permute-done.other, bf16[384,2048]{1,0:T(8,128)(2,1)S(1)} %copy-done.1), custom_call_target="tpu_custom_call" | custom-call | tf_op jit(solution)/shard_map/add/pallas_call | solution.py:129
Async XLA Ops:
  0.6 65.6 %copy-start = (bf16[1,1,256,2048]{3,2,1,0:T(8,128)(2,1)S(1)}, bf16[1,1,256,2048]{3,2,1,0:T(8,128)(2,1)}, u32[]{:S(2)}) copy-start(bf16[1,1,256,2048]{3,2,1,0:T(8,128)(2,1)} %param.9) | copy-start | bytes 3145732
  22.9 43.4 %copy-start.1 = (bf16[384,2048]{1,0:T(8,128)(2,1)S(1)}, bf16[384,2048]{1,0:T(8,128)(2,1)}, u32[]{:S(2)}) copy-start(bf16[384,2048]{1,0:T(8,128)(2,1)} %base.1) | copy-start | bytes 4718596
  60.7 7.5 %collective-permute-start = (bf16[8,8,3,16,128]{4,3,2,1,0:T(8,128)(2,1)S(1)}, bf16[8,8,3,16,128]{4,3,2,1,0:T(8,128)(2,1)S(1)}, u32[]{:S(2)}, u32[]{:S(2)}) collective-permute-start(bf16[8,8,3,16,128]{4,3,2,1,0:T(8,128)(2,1)S(1)} %all_to_all.17.mine), channel_id=1, source_target_pairs={{0,32},{32,0},{1,33},{33,1},{2,34},{34,2},{3,35},{35,3},{4,36},{36... | collective-permute-start | bytes 2359304 | tf_op jit(solution)/shard_map/ppermute | solution.py:168

commit v5 on v4

--- a/solution.py
+++ b/solution.py
@@ -26,13 +26,6 @@
         self.g = at["zl"] * 8 + at["x"] * 2 + at["c"]
         self.col = at["zh"] * 4 + at["ya"] * 2 + at["yb"]
         self.s = 2 * self.col + at["yc"]
-
-
-def run_of(lengths, s, g):
-    start = jnp.int32(0)
-    for i in range(GROUPS):
-        start += jnp.where(i < g, lengths[i, s], 0)
-    return start, lengths[g, s]
 
 
 def encode_kernel(lengths_in, slots_in, master_in, sent_in, out, lengths_out, slots_out, lengths, master, sent, sems):
@@ -48,10 +41,12 @@
         load.start()
     at = Place()
     loads[0].wait()
-    start, count = run_of(lengths, at.s, at.g)
+    start = jnp.int32(0)
+    for n in range(GROUPS - 1):
+        start += jnp.where(n < at.g, lengths[n, at.s], 0)
+    for load in loads[3:]:
+        load.wait()
     for j in range(MOST):
-        loads[3 + 2 * j].wait()
-        loads[4 + 2 * j].wait()
         change = master[j] - sent[j].astype(jnp.float32)
         mean = jnp.sum(change * change, axis=(0, 1), keepdims=True) * (1.0 / (BLK * BLK))
         scale = jnp.sqrt(mean + EPSILON).astype(jnp.bfloat16).astype(jnp.float32)
@@ -60,12 +55,9 @@
         r = lax.rem(start + j, TROWS)
         k, i = lax.div(r, 3), lax.rem(r, 3)
         to = ((k >> 1) ^ at.yb) * 4 + (k & 1)
-
-        @pl.when(j < count)
-        def _():
-            for n in range(8):
-                peer = (n >> 1 & 1) * 16 + (n & 1) * 8 + (n >> 2) * 2
-                out[peer + to, i] = value[n * PART : (n + 1) * PART, :]
+        for n in range(8):
+            peer = (n >> 1 & 1) * 16 + (n & 1) * 8 + (n >> 2) * 2
+            out[peer + to, i] = value[n * PART : (n + 1) * PART, :]
 
     loads[1].wait()
     loads[2].wait()
@@ -102,20 +94,29 @@
                 out[to, n, i] = part
 
 
-def add_kernel(mine, other, base, out):
-    at = Place()
-    near = at.c == 0
-    for col in range(16):
-        cols = pl.ds(col * BLK, BLK)
-        side = (col & 1) ^ at.yb
+def add_half(half, tiles, base, out, done, sems):
+    at = Place()
+    stores = []
+    for i in range(3):
+        first = pl.multiple_of(i * BLK + half(at.c) * HALF, HALF)
         for n in range(4):
-            chip = 2 * n + side
-            for i in range(3):
-                a, b = mine[chip, col >> 1, i], other[chip, col >> 1, i]
-                for half in range(2):
-                    part = (jnp.where(near, b, a) if half else jnp.where(near, a, b)).astype(jnp.float32)
-                    rows = pl.ds(i * BLK + half * HALF + n * PART, PART)
-                    out[rows, cols] = (base[rows, cols].astype(jnp.float32) + part).astype(jnp.bfloat16)
+            rows = pl.ds(pl.multiple_of(first + n * PART, PART), PART)
+            for col in range(16):
+                cols = pl.ds(col * BLK, BLK)
+                part = tiles[2 * n + ((col & 1) ^ at.yb), col >> 1, i].astype(jnp.float32)
+                done[i, n * PART : (n + 1) * PART, cols] = (base[rows, cols].astype(jnp.float32) + part).astype(jnp.bfloat16)
+        stores.append(pltpu.make_async_copy(done.at[i], out.at[pl.ds(first, HALF)], sems.at[i]))
+        stores[i].start()
+    for store in stores:
+        store.wait()
+
+
+def add_mine_kernel(mine, base, out, done, sems):
+    add_half(lambda c: c, mine, base, out, done, sems)
+
+
+def add_other_kernel(other, base, begun, out, done, sems):
+    add_half(lambda c: 1 - c, other, base, out, done, sems)
 
 
 SMEM = pl.BlockSpec(memory_space=pltpu.SMEM)
@@ -134,6 +135,19 @@
         compiler_params=LIMIT,
         name=name,
     )(*args)
+
+
+def add_call(kernel, name, tiles, base, *begun):
+    return pl.pallas_call(
+        kernel,
+        out_shape=jax.typeof(base),
+        in_specs=[VMEM, VMEM] + [HBM] * len(begun),
+        out_specs=HBM,
+        scratch_shapes=[pltpu.VMEM((3, HALF, base.shape[1]), jnp.bfloat16), pltpu.SemaphoreType.DMA((3,))],
+        input_output_aliases={2: 0} if begun else {},
+        compiler_params=LIMIT,
+        name=name,
+    )(tiles, base, *begun)
 
 
 def exchange(x, axes):
@@ -169,9 +183,8 @@
     in_flight = lax.dot_general(
         tokens[0, 0], rollout_base, (((1,), (1,)), ((), ())), preferred_element_type=jnp.float32
     ).astype(jnp.bfloat16)[None, None]
-    (new_weights,) = call(
-        add_kernel, "add", [VMEM, VMEM, VMEM], [rollout_base.shape], mine, other, rollout_base
-    )
+    begun = add_call(add_mine_kernel, "add_mine", mine, rollout_base)
+    new_weights = add_call(add_other_kernel, "add_other", other, rollout_base, begun)
     return (new_weights, in_flight)
 
 

time: 70.2 us -> 69.4 us (0.989)
    pallas_call x0 -> x2, Pallas kernels: none -> 1.96 us  [add_call(): pl.pallas_call(kernel, out_shape=jax.typeof(base), in_specs=[VMEM, VMEM]...]
    pallas_call x3 -> x2, Pallas kernels: 3.12 us -> 1.34 us  [call(): pl.pallas_call(kernel, out_shape=outs, in_specs=specs, out_specs=(VMEM,)...]
  transfers between devices with their start and end apart: 1 -> 1, of which waited for: 1 -> 0; matrix products, arithmetic and copies ran while one was open for 2% -> 2% of each run, Pallas kernels for 0% -> 1%
where the time goes in v5:
time: 69.4 us; the launch traced here: 69.1 us
  blocking collectives  56.5 us (81%)
  starting transfers between devices  5.58 us (8%)
  Pallas kernels  4.88 us (7%)
  matrix products  1.41 us (2%)
  between operations  0.71 us (1%)
    all_to_all x3, blocking collectives, exchange(): return lax.all_to_all(x, axes, split_axis=0, concat_axis=0, tiled=True)  56.5 us
    ppermute x1, starting transfers between devices, shards(): other = lax.ppermute(mine, 'c', [(0, 1), (1, 0)])  5.58 us
    pallas_call x2, Pallas kernels, add_call(): pl.pallas_call(kernel, out_shape=jax.typeof(base), in_specs=[VMEM, VMEM]...  1.96 us
    pallas_call x1, Pallas kernels, shards(): pl.pallas_call(encode_kernel, out_shape=(jax.ShapeDtypeStruct((32, 3, PAR...  1.58 us
    dot_general x1, matrix products, shards(): lax.dot_general(tokens[0, 0], rollout_base, (((1,), (1,)), ((), ())), pre...  1.41 us
  transfers between devices with their start and end apart: 1, of which 0 were waited for; matrix products, arithmetic and copies ran while one was open for 2% of the time, Pallas kernels for 1%

profile of v5, /device:TPU:1, one launch (start us, length us, event | category | flops | bytes accessed | tf_op | source)
XLA Modules:
  0.0 69.1 jit_solution(10294112343130869656)
XLA Ops:
  0.6 0.0 copy-start
  0.6 1.6 %encode.1 = (bf16[32,3,16,128]{3,2,1,0:T(8,128)(2,1)S(1)}, s32[16,32]{1,0:T(8,128)S(1)}, s32[8]{0:T(128)S(1)}) custom-call(s32[16,32]{1,0:T(8,128)} %bitcast.7, s32[8]{0:T(128)} %slots_in.1, f32[1,6,128,128]{3,2,1,0:T(8,128)} %master_in.1, bf16[1,6,128,128]{3,2,1,0:T(8,128)(2,1)} %sent_in.1), custom_call_target="tpu_custom_call" | custom-call | tf_op jit(solution)/shard_map/encode/pallas_call | solution.py:159
  2.2 18.9 %all_to_all.15.got = bf16[32,3,16,128]{3,2,1,0:T(8,128)(2,1)S(1)} all-to-all(bf16[32,3,16,128]{3,2,1,0:T(8,128)(2,1)S(1)} %get-tuple-element.7), channel_id=1, replica_groups=mesh['zl'=2,'x'=4,'c'=2,'zh'=4,'ya'=2,'yb'=2,'yc'=2] {'zl','x','c','yc'}, dimensions={0} | all-to-all | bytes 786432 | tf_op jit(solution)/shard_map/all_to_all | solution.py:154
  21.1 1.2 %slot.1 = bf16[16,3,16,128]{3,2,1,0:T(8,128)(2,1)S(1)} custom-call(s32[16,32]{1,0:T(8,128)S(1)} %get-tuple-element.5.lengths, s32[8]{0:T(128)S(1)} %get-tuple-element.6.slots, bf16[32,3,16,128]{3,2,1,0:T(8,128)(2,1)S(1)} %all_to_all.15.got), custom_call_target="tpu_custom_call" | custom-call | tf_op jit(solution)/shard_map/slot/pallas_call | solution.py:130
  22.4 0.0 copy-start.1
  22.4 24.0 %all_to_all.16.got = bf16[16,3,16,128]{3,2,1,0:T(8,128)(2,1)S(1)} all-to-all(bf16[16,3,16,128]{3,2,1,0:T(8,128)(2,1)S(1)} %slot.1), channel_id=1, replica_groups=mesh['zl'=2,'x'=4,'c'=2,'zh'=4,'ya'=2,'yb'=2,'yc'=2] {'zh','ya','yb'}, dimensions={0} | all-to-all | bytes 393216 | tf_op jit(solution)/shard_map/all_to_all | solution.py:154
  46.4 0.1 spread.1
  46.5 13.6 %all_to_all.17.mine = bf16[8,8,3,16,128]{4,3,2,1,0:T(8,128)(2,1)S(1)} all-to-all(bf16[8,8,3,16,128]{4,3,2,1,0:T(8,128)(2,1)S(1)} %spread.1), channel_id=1, replica_groups=mesh['zl'=2,'x'=4,'c'=2,'zh'=4,'ya'=2,'yb'=2,'yc'=2] {'zl','x'}, dimensions={0} | all-to-all | bytes 1572864 | tf_op jit(solution)/shard_map/all_to_all | solution.py:154
  60.1 5.6 %collective-permute-start = (bf16[8,8,3,16,128]{4,3,2,1,0:T(8,128)(2,1)S(1)}, bf16[8,8,3,16,128]{4,3,2,1,0:T(8,128)(2,1)S(1)}, u32[]{:S(2)}, u32[]{:S(2)}) collective-permute-start(bf16[8,8,3,16,128]{4,3,2,1,0:T(8,128)(2,1)S(1)} %all_to_all.17.mine), channel_id=1, source_target_pairs={{0,32},{32,0},{1,33},{33,1},{2,34},{34,2},{3,35},{35,3},{4,36},{36... | collective-permute-start | bytes 2359304 | tf_op jit(solution)/shard_map/ppermute | solution.py:182
  65.7 0.0 copy-done
  65.7 0.0 copy-done.1
  65.8 1.4 %fusion = bf16[1,1,256,384]{3,2,1,0:T(8,128)(2,1)} fusion(bf16[384,2048]{1,0:T(8,128)(2,1)S(1)} %copy-done.1, bf16[1,1,256,2048]{3,2,1,0:T(8,128)(2,1)S(1)} %copy-done), kind=kOutput, calls=%fused_computation.1 | convolution fusion | flops 402751488 | bytes 2818048 | tf_op jit(solution)/shard_map/dot_general | solution.py:183
  67.2 1.0 %add_mine.1.begun = bf16[384,2048]{1,0:T(8,128)(2,1)} custom-call(bf16[8,8,3,16,128]{4,3,2,1,0:T(8,128)(2,1)S(1)} %all_to_all.17.mine, bf16[384,2048]{1,0:T(8,128)(2,1)S(1)} %copy-done.1), custom_call_target="tpu_custom_call" | custom-call | tf_op jit(solution)/shard_map/add_mine/pallas_call | solution.py:141
  68.1 0.0 collective-permute-done.other
  68.1 1.0 %add_other.1 = bf16[384,2048]{1,0:T(8,128)(2,1)} custom-call(bf16[8,8,3,16,128]{4,3,2,1,0:T(8,128)(2,1)S(1)} %collective-permute-done.other, bf16[384,2048]{1,0:T(8,128)(2,1)S(1)} %copy-done.1, bf16[384,2048]{1,0:T(8,128)(2,1)} %add_mine.1.begun), custom_call_target="tpu_custom_call", output_to_operand_aliasing={{}: (2, {})} | custom-call | tf_op jit(solution)/shard_map/add_other/pallas_call | solution.py:141
Async XLA Ops:
  0.6 65.1 %copy-start = (bf16[1,1,256,2048]{3,2,1,0:T(8,128)(2,1)S(1)}, bf16[1,1,256,2048]{3,2,1,0:T(8,128)(2,1)}, u32[]{:S(2)}) copy-start(bf16[1,1,256,2048]{3,2,1,0:T(8,128)(2,1)} %param.9) | copy-start | bytes 3145732
  22.4 43.4 %copy-start.1 = (bf16[384,2048]{1,0:T(8,128)(2,1)S(1)}, bf16[384,2048]{1,0:T(8,128)(2,1)}, u32[]{:S(2)}) copy-start(bf16[384,2048]{1,0:T(8,128)(2,1)} %base.3) | copy-start | bytes 4718596
  60.1 8.0 %collective-permute-start = (bf16[8,8,3,16,128]{4,3,2,1,0:T(8,128)(2,1)S(1)}, bf16[8,8,3,16,128]{4,3,2,1,0:T(8,128)(2,1)S(1)}, u32[]{:S(2)}, u32[]{:S(2)}) collective-permute-start(bf16[8,8,3,16,128]{4,3,2,1,0:T(8,128)(2,1)S(1)} %all_to_all.17.mine), channel_id=1, source_target_pairs={{0,32},{32,0},{1,33},{33,1},{2,34},{34,2},{3,35},{35,3},{4,36},{36... | collective-permute-start | bytes 2359304 | tf_op jit(solution)/shard_map/ppermute | solution.py:182

commit v6 on v5

--- a/solution.py
+++ b/solution.py
@@ -54,44 +54,42 @@
         value = (encoded.astype(jnp.float32) * scale).astype(jnp.bfloat16)
         r = lax.rem(start + j, TROWS)
         k, i = lax.div(r, 3), lax.rem(r, 3)
-        to = ((k >> 1) ^ at.yb) * 4 + (k & 1)
+        to = (((k >> 1) + i + at.yb) & 1) * 4 + (k & 1)
+        slot = 0 if j < 2 else 1 if j == 5 else i >> 1
         for n in range(8):
             peer = (n >> 1 & 1) * 16 + (n & 1) * 8 + (n >> 2) * 2
-            out[peer + to, i] = value[n * PART : (n + 1) * PART, :]
+            out[peer + to, slot] = value[n * PART : (n + 1) * PART, :]
 
     loads[1].wait()
     loads[2].wait()
 
 
-def slot_kernel(lengths, slots, got, out):
-    at = Place()
-    kb = (at.x & 1) ^ at.yb
-    first = 3 * (2 * kb + at.yc)
-    ends = []
+def slot_kernel(lengths, slots, got, out, table):
+    at = Place()
     for side in range(2):
-        end, row = jnp.int32(0), []
-        for n in range(GROUPS - 1):
-            end += lengths[n, 2 * at.col + side]
-            row.append(end)
-        ends.append(row)
+        start = jnp.int32(0)
+        for n in range(GROUPS):
+            for j in range(MOST):
+                table[side, start + j] = n * 8 + j
+            start += lengths[n, 2 * at.col + side]
+    odd = (at.x + at.yb) & 1
     for e in range(EXPERTS):
-        to = 2 * slots[e] + kb
+        p = slots[e]
         for i in range(3):
-            q = (e % 4) * TROWS + first + i
-            owner = jnp.int32(0)
-            for end in ends[e // 4]:
-                owner += jnp.where(end <= q, 1, 0)
-            out[to, i] = got[2 * owner + e // 4, i]
+            kb = odd ^ (i & 1)
+            entry = table[e // 4, (e % 4) * TROWS + 6 * kb + 3 * at.yc + i]
+            slot = jnp.where((entry & 7) >= (2 if i == 2 else 5), 1, 0)
+            out[2 * p + kb, i >> 1] = got[(entry >> 3) * 2 + e // 4, slot]
 
 
 def spread_kernel(got, out):
     at = Place()
-    side = (at.x & 1) ^ at.yb
+    side = (at.x + at.yb) & 1
     for n in range(8):
-        for i in range(3):
-            part = got[2 * n + side, i]
-            for to in range(8):
-                out[to, n, i] = part
+        parts = (got[2 * n + side, 0], got[2 * n + side, 1], got[2 * n + 1 - side, 0])
+        for to in range(8):
+            for m in range(3):
+                out[to, n, m] = parts[m]
 
 
 def add_half(half, tiles, base, out, done, sems):
@@ -103,7 +101,7 @@
             rows = pl.ds(pl.multiple_of(first + n * PART, PART), PART)
             for col in range(16):
                 cols = pl.ds(col * BLK, BLK)
-                part = tiles[2 * n + ((col & 1) ^ at.yb), col >> 1, i].astype(jnp.float32)
+                part = tiles[2 * n + ((at.yb + i + col) & 1), col >> 1, (0, 2, 1)[i]].astype(jnp.float32)
                 done[i, n * PART : (n + 1) * PART, cols] = (base[rows, cols].astype(jnp.float32) + part).astype(jnp.bfloat16)
         stores.append(pltpu.make_async_copy(done.at[i], out.at[pl.ds(first, HALF)], sems.at[i]))
         stores[i].start()
@@ -125,13 +123,14 @@
 LIMIT = pltpu.CompilerParams(vmem_limit_bytes=32 * 1024 * 1024)
 
 
-def call(kernel, name, specs, shapes, *args):
+def call(kernel, name, specs, shapes, *args, scratch=()):
     outs = tuple(jax.ShapeDtypeStruct(s, jnp.bfloat16) for s in shapes)
     return pl.pallas_call(
         kernel,
         out_shape=outs,
         in_specs=specs,
         out_specs=(VMEM,) * len(outs),
+        scratch_shapes=scratch,
         compiler_params=LIMIT,
         name=name,
     )(*args)
@@ -159,7 +158,7 @@
     out, lengths, expert_slot = pl.pallas_call(
         encode_kernel,
         out_shape=(
-            jax.ShapeDtypeStruct((32, 3, PART, BLK), jnp.bfloat16),
+            jax.ShapeDtypeStruct((32, 2, PART, BLK), jnp.bfloat16),
             jax.typeof(lengths),
             jax.typeof(expert_slot),
         ),
@@ -175,7 +174,10 @@
         name="encode",
     )(*(pltpu.with_memory_space_constraint(v, pltpu.HBM) for v in (lengths, expert_slot, master_new, sent_base)))
     out = exchange(out, ("zl", "x", "c", "yc"))
-    (out,) = call(slot_kernel, "slot", [SMEM, SMEM, VMEM], [(16, 3, PART, BLK)], lengths, expert_slot, out)
+    (out,) = call(
+        slot_kernel, "slot", [SMEM, SMEM, VMEM], [(16, 2, PART, BLK)], lengths, expert_slot, out,
+        scratch=[pltpu.SMEM((2, 64), jnp.int32)],
+    )
     out = exchange(out, ("zh", "ya", "yb"))
     (out,) = call(spread_kernel, "spread", [VMEM], [(8, 8, 3, PART, BLK)], out)
     mine = exchange(out, ("zl", "x"))

time: 69.4 us -> 67 us (0.965)
  blocking collectives: 56.5 us -> 54.2 us
    all_to_all x3, blocking collectives: 56.5 us -> 54.2 us  [exchange(): return lax.all_to_all(x, axes, split_axis=0, concat_axis=0, tiled=True)]
where the time goes in v6:
time: 67 us; the launch traced here: 66.8 us
  blocking collectives  54.2 us (81%)
  starting transfers between devices  5.6 us (8%)
  Pallas kernels  4.79 us (7%)
  matrix products  1.41 us (2%)
  between operations  0.71 us (1%)
    all_to_all x3, blocking collectives, exchange(): return lax.all_to_all(x, axes, split_axis=0, concat_axis=0, tiled=True)  54.2 us
    ppermute x1, starting transfers between devices, shards(): other = lax.ppermute(mine, 'c', [(0, 1), (1, 0)])  5.6 us
    pallas_call x2, Pallas kernels, add_call(): pl.pallas_call(kernel, out_shape=jax.typeof(base), in_specs=[VMEM, VMEM]...  1.98 us
    pallas_call x1, Pallas kernels, shards(): pl.pallas_call(encode_kernel, out_shape=(jax.ShapeDtypeStruct((32, 2, PAR...  1.58 us
    dot_general x1, matrix products, shards(): lax.dot_general(tokens[0, 0], rollout_base, (((1,), (1,)), ((), ())), pre...  1.41 us
  transfers between devices with their start and end apart: 1, of which 0 were waited for; matrix products, arithmetic and copies ran while one was open for 2% of the time, Pallas kernels for 1%

profile of v6, /device:TPU:1, one launch (start us, length us, event | category | flops | bytes accessed | tf_op | source)
XLA Modules:
  0.0 66.8 jit_solution(14174411266694220285)
XLA Ops:
  0.6 0.0 copy-start
  0.6 1.6 %encode.1 = (bf16[32,2,16,128]{3,2,1,0:T(8,128)(2,1)S(1)}, s32[16,32]{1,0:T(8,128)S(1)}, s32[8]{0:T(128)S(1)}) custom-call(s32[16,32]{1,0:T(8,128)} %bitcast.7, s32[8]{0:T(128)} %slots_in.1, f32[1,6,128,128]{3,2,1,0:T(8,128)} %master_in.1, bf16[1,6,128,128]{3,2,1,0:T(8,128)(2,1)} %sent_in.1), custom_call_target="tpu_custom_call" | custom-call | tf_op jit(solution)/shard_map/encode/pallas_call | solution.py:158
  2.2 17.8 %all_to_all.15.got = bf16[32,2,16,128]{3,2,1,0:T(8,128)(2,1)S(1)} all-to-all(bf16[32,2,16,128]{3,2,1,0:T(8,128)(2,1)S(1)} %get-tuple-element.7), channel_id=1, replica_groups=mesh['zl'=2,'x'=4,'c'=2,'zh'=4,'ya'=2,'yb'=2,'yc'=2] {'zl','x','c','yc'}, dimensions={0} | all-to-all | bytes 524288 | tf_op jit(solution)/shard_map/all_to_all | solution.py:153
  20.0 0.0 copy-start.1
  20.0 1.1 %slot.1 = bf16[16,2,16,128]{3,2,1,0:T(8,128)(2,1)S(1)} custom-call(s32[16,32]{1,0:T(8,128)S(1)} %get-tuple-element.5.lengths, s32[8]{0:T(128)S(1)} %get-tuple-element.6.slots, bf16[32,2,16,128]{3,2,1,0:T(8,128)(2,1)S(1)} %all_to_all.15.got), custom_call_target="tpu_custom_call" | custom-call | tf_op jit(solution)/shard_map/slot/pallas_call | solution.py:128
  21.1 23.8 %all_to_all.16.got = bf16[16,2,16,128]{3,2,1,0:T(8,128)(2,1)S(1)} all-to-all(bf16[16,2,16,128]{3,2,1,0:T(8,128)(2,1)S(1)} %slot.1), channel_id=1, replica_groups=mesh['zl'=2,'x'=4,'c'=2,'zh'=4,'ya'=2,'yb'=2,'yc'=2] {'zh','ya','yb'}, dimensions={0} | all-to-all | bytes 262144 | tf_op jit(solution)/shard_map/all_to_all | solution.py:153
  45.0 0.1 spread.1
  45.1 12.6 %all_to_all.17.mine = bf16[8,8,3,16,128]{4,3,2,1,0:T(8,128)(2,1)S(1)} all-to-all(bf16[8,8,3,16,128]{4,3,2,1,0:T(8,128)(2,1)S(1)} %spread.1), channel_id=1, replica_groups=mesh['zl'=2,'x'=4,'c'=2,'zh'=4,'ya'=2,'yb'=2,'yc'=2] {'zl','x'}, dimensions={0} | all-to-all | bytes 1572864 | tf_op jit(solution)/shard_map/all_to_all | solution.py:153
  57.7 5.6 %collective-permute-start = (bf16[8,8,3,16,128]{4,3,2,1,0:T(8,128)(2,1)S(1)}, bf16[8,8,3,16,128]{4,3,2,1,0:T(8,128)(2,1)S(1)}, u32[]{:S(2)}, u32[]{:S(2)}) collective-permute-start(bf16[8,8,3,16,128]{4,3,2,1,0:T(8,128)(2,1)S(1)} %all_to_all.17.mine), channel_id=1, source_target_pairs={{0,32},{32,0},{1,33},{33,1},{2,34},{34,2},{3,35},{35,3},{4,36},{36... | collective-permute-start | bytes 2359304 | tf_op jit(solution)/shard_map/ppermute | solution.py:184
  63.3 0.0 copy-done
  63.3 0.0 copy-done.1
  63.4 1.4 %fusion = bf16[1,1,256,384]{3,2,1,0:T(8,128)(2,1)} fusion(bf16[384,2048]{1,0:T(8,128)(2,1)S(1)} %copy-done.1, bf16[1,1,256,2048]{3,2,1,0:T(8,128)(2,1)S(1)} %copy-done), kind=kOutput, calls=%fused_computation.1 | convolution fusion | flops 402751488 | bytes 2818048 | tf_op jit(solution)/shard_map/dot_general | solution.py:185
  64.8 1.0 %add_mine.1.begun = bf16[384,2048]{1,0:T(8,128)(2,1)} custom-call(bf16[8,8,3,16,128]{4,3,2,1,0:T(8,128)(2,1)S(1)} %all_to_all.17.mine, bf16[384,2048]{1,0:T(8,128)(2,1)S(1)} %copy-done.1), custom_call_target="tpu_custom_call" | custom-call | tf_op jit(solution)/shard_map/add_mine/pallas_call | solution.py:140
  65.7 0.0 collective-permute-done.other
  65.8 1.0 %add_other.1 = bf16[384,2048]{1,0:T(8,128)(2,1)} custom-call(bf16[8,8,3,16,128]{4,3,2,1,0:T(8,128)(2,1)S(1)} %collective-permute-done.other, bf16[384,2048]{1,0:T(8,128)(2,1)S(1)} %copy-done.1, bf16[384,2048]{1,0:T(8,128)(2,1)} %add_mine.1.begun), custom_call_target="tpu_custom_call", output_to_operand_aliasing={{}: (2, {})} | custom-call | tf_op jit(solution)/shard_map/add_other/pallas_call | solution.py:140
Async XLA Ops:
  0.6 62.7 %copy-start = (bf16[1,1,256,2048]{3,2,1,0:T(8,128)(2,1)S(1)}, bf16[1,1,256,2048]{3,2,1,0:T(8,128)(2,1)}, u32[]{:S(2)}) copy-start(bf16[1,1,256,2048]{3,2,1,0:T(8,128)(2,1)} %param.9) | copy-start | bytes 3145732
  20.0 43.4 %copy-start.1 = (bf16[384,2048]{1,0:T(8,128)(2,1)S(1)}, bf16[384,2048]{1,0:T(8,128)(2,1)}, u32[]{:S(2)}) copy-start(bf16[384,2048]{1,0:T(8,128)(2,1)} %base.3) | copy-start | bytes 4718596
  57.7 8.0 %collective-permute-start = (bf16[8,8,3,16,128]{4,3,2,1,0:T(8,128)(2,1)S(1)}, bf16[8,8,3,16,128]{4,3,2,1,0:T(8,128)(2,1)S(1)}, u32[]{:S(2)}, u32[]{:S(2)}) collective-permute-start(bf16[8,8,3,16,128]{4,3,2,1,0:T(8,128)(2,1)S(1)} %all_to_all.17.mine), channel_id=1, source_target_pairs={{0,32},{32,0},{1,33},{33,1},{2,34},{34,2},{3,35},{35,3},{4,36},{36... | collective-permute-start | bytes 2359304 | tf_op jit(solution)/shard_map/ppermute | solution.py:184

commit v7 on v6

--- a/solution.py
+++ b/solution.py
@@ -1,5 +1,6 @@
 import jax
 import jax.numpy as jnp
+import numpy as np
 from jax import lax
 from jax.experimental import pallas as pl
 from jax.experimental.pallas import tpu as pltpu
@@ -24,6 +25,7 @@
         at = {name: lax.axis_index(name) for name in AXES}
         self.c, self.x, self.yb, self.yc = at["c"], at["x"], at["yb"], at["yc"]
         self.g = at["zl"] * 8 + at["x"] * 2 + at["c"]
+        self.turn = (at["zh"] >> 1) ^ (at["zh"] & 1)
         self.col = at["zh"] * 4 + at["ya"] * 2 + at["yb"]
         self.s = 2 * self.col + at["yc"]
 
@@ -57,7 +59,7 @@
         to = (((k >> 1) + i + at.yb) & 1) * 4 + (k & 1)
         slot = 0 if j < 2 else 1 if j == 5 else i >> 1
         for n in range(8):
-            peer = (n >> 1 & 1) * 16 + (n & 1) * 8 + (n >> 2) * 2
+            peer = ((n >> 1 & 1) ^ at.turn) * 16 + (n & 1) * 8 + (n >> 2) * 2
             out[peer + to, slot] = value[n * PART : (n + 1) * PART, :]
 
     loads[1].wait()
@@ -92,29 +94,38 @@
                 out[to, n, m] = parts[m]
 
 
-def add_half(half, tiles, base, out, done, sems):
+def add_rows(at, half, i, tiles, base, new):
+    for n in range(4):
+        rows = pl.ds(pl.multiple_of(i * BLK + half * HALF + n * PART, PART), PART)
+        for col in range(16):
+            cols = pl.ds(col * BLK, BLK)
+            chip = 4 * ((n >> 1) ^ at.turn) + 2 * (n & 1) + ((at.yb + i + col) & 1)
+            part = tiles[chip, col >> 1, (0, 2, 1)[i]].astype(jnp.float32)
+            new[i, n * PART : (n + 1) * PART, cols] = (base[rows, cols].astype(jnp.float32) + part).astype(jnp.bfloat16)
+
+
+def add_mine_kernel(mine, base, new):
+    at = Place()
+    for i in range(3):
+        add_rows(at, at.c, i, mine, base, new)
+
+
+def add_other_kernel(other, base, new_mine, out, new, sems):
     at = Place()
     stores = []
+
+    def store(half, i, rows):
+        first = pl.multiple_of(i * BLK + half * HALF, HALF)
+        stores.append(pltpu.make_async_copy(rows.at[i], out.at[pl.ds(first, HALF)], sems.at[len(stores)]))
+        stores[-1].start()
+
     for i in range(3):
-        first = pl.multiple_of(i * BLK + half(at.c) * HALF, HALF)
-        for n in range(4):
-            rows = pl.ds(pl.multiple_of(first + n * PART, PART), PART)
-            for col in range(16):
-                cols = pl.ds(col * BLK, BLK)
-                part = tiles[2 * n + ((at.yb + i + col) & 1), col >> 1, (0, 2, 1)[i]].astype(jnp.float32)
-                done[i, n * PART : (n + 1) * PART, cols] = (base[rows, cols].astype(jnp.float32) + part).astype(jnp.bfloat16)
-        stores.append(pltpu.make_async_copy(done.at[i], out.at[pl.ds(first, HALF)], sems.at[i]))
-        stores[i].start()
-    for store in stores:
-        store.wait()
-
-
-def add_mine_kernel(mine, base, out, done, sems):
-    add_half(lambda c: c, mine, base, out, done, sems)
-
-
-def add_other_kernel(other, base, begun, out, done, sems):
-    add_half(lambda c: 1 - c, other, base, out, done, sems)
+        store(at.c, i, new_mine)
+    for i in range(3):
+        add_rows(at, 1 - at.c, i, other, base, new)
+        store(1 - at.c, i, new)
+    for started in stores:
+        started.wait()
 
 
 SMEM = pl.BlockSpec(memory_space=pltpu.SMEM)
@@ -136,21 +147,17 @@
     )(*args)
 
 
-def add_call(kernel, name, tiles, base, *begun):
-    return pl.pallas_call(
-        kernel,
-        out_shape=jax.typeof(base),
-        in_specs=[VMEM, VMEM] + [HBM] * len(begun),
-        out_specs=HBM,
-        scratch_shapes=[pltpu.VMEM((3, HALF, base.shape[1]), jnp.bfloat16), pltpu.SemaphoreType.DMA((3,))],
-        input_output_aliases={2: 0} if begun else {},
-        compiler_params=LIMIT,
-        name=name,
-    )(tiles, base, *begun)
-
-
 def exchange(x, axes):
     return lax.all_to_all(x, axes, split_axis=0, concat_axis=0, tiled=True)
+
+
+def turned_groups():
+    sizes = tuple(AXES.values())
+    groups = []
+    for side, x, c, yc in np.ndindex(2, 4, 2, 2):
+        members = [(side ^ (zh >> 1) ^ (zh & 1), x, c, zh, ya, yb, yc) for zh, ya, yb in np.ndindex(4, 2, 2)]
+        groups.append([int(np.ravel_multi_index(member, sizes)) for member in members])
+    return groups
 
 
 def shards(master_new, sent_base, rollout_base, tokens, lengths, expert_slot):
@@ -178,15 +185,26 @@
         slot_kernel, "slot", [SMEM, SMEM, VMEM], [(16, 2, PART, BLK)], lengths, expert_slot, out,
         scratch=[pltpu.SMEM((2, 64), jnp.int32)],
     )
-    out = exchange(out, ("zh", "ya", "yb"))
+    out = lax.all_to_all(
+        out, tuple(AXES), split_axis=0, concat_axis=0, tiled=True, axis_index_groups=turned_groups()
+    )
     (out,) = call(spread_kernel, "spread", [VMEM], [(8, 8, 3, PART, BLK)], out)
     mine = exchange(out, ("zl", "x"))
     other = lax.ppermute(mine, "c", [(0, 1), (1, 0)])
     in_flight = lax.dot_general(
         tokens[0, 0], rollout_base, (((1,), (1,)), ((), ())), preferred_element_type=jnp.float32
     ).astype(jnp.bfloat16)[None, None]
-    begun = add_call(add_mine_kernel, "add_mine", mine, rollout_base)
-    new_weights = add_call(add_other_kernel, "add_other", other, rollout_base, begun)
+    half = (3, HALF, rollout_base.shape[1])
+    (new_mine,) = call(add_mine_kernel, "add_mine", [VMEM] * 2, [half], mine, rollout_base)
+    new_weights = pl.pallas_call(
+        add_other_kernel,
+        out_shape=jax.typeof(rollout_base),
+        in_specs=[VMEM] * 3,
+        out_specs=HBM,
+        scratch_shapes=[pltpu.VMEM(half, jnp.bfloat16), pltpu.SemaphoreType.DMA((6,))],
+        compiler_params=LIMIT,
+        name="add_other",
+    )(other, rollout_base, new_mine)
     return (new_weights, in_flight)
 
 

time: 67 us -> 66.4 us (level)
    all_to_all x0 -> x1, blocking collectives: none -> 23.1 us  [shards(): lax.all_to_all(out, tuple(AXES), split_axis=0, concat_axis=0, tiled=True,...]
    all_to_all x3 -> x2, blocking collectives: 54.2 us -> 31.5 us  [exchange(): return lax.all_to_all(x, axes, split_axis=0, concat_axis=0, tiled=True)]
    pallas_call x2 -> x1, Pallas kernels: 1.98 us -> 1.18 us  [shards(): pl.pallas_call(add_other_kernel, out_shape=jax.typeof(rollout_base), in_s...]
    pallas_call x2 -> x3, Pallas kernels: 1.24 us -> 1.45 us  [call(): pl.pallas_call(kernel, out_shape=outs, in_specs=specs, out_specs=(VMEM,)...]
  transfers between devices with their start and end apart: 1 -> 1, of which waited for: 0 -> 1; matrix products, arithmetic and copies ran while one was open for 2% -> 2% of each run, Pallas kernels for 1% -> 0%
where the time goes in v7:
time: 66.4 us; the launch traced here: 66.1 us
  blocking collectives  54.6 us (82%)
  starting transfers between devices  4.98 us (8%)
  Pallas kernels  4.21 us (6%)
  matrix products  1.41 us (2%)
  between operations  0.7 us (1%)
    all_to_all x2, blocking collectives, exchange(): return lax.all_to_all(x, axes, split_axis=0, concat_axis=0, tiled=True)  31.5 us
    all_to_all x1, blocking collectives, shards(): lax.all_to_all(out, tuple(AXES), split_axis=0, concat_axis=0, tiled=True,...  23.1 us
    ppermute x1, starting transfers between devices, shards(): other = lax.ppermute(mine, 'c', [(0, 1), (1, 0)])  4.98 us
    pallas_call x1, Pallas kernels, shards(): pl.pallas_call(encode_kernel, out_shape=(jax.ShapeDtypeStruct((32, 2, PAR...  1.58 us
    pallas_call x3, Pallas kernels, call(): pl.pallas_call(kernel, out_shape=outs, in_specs=specs, out_specs=(VMEM,)...  1.45 us
    dot_general x1, matrix products, shards(): lax.dot_general(tokens[0, 0], rollout_base, (((1,), (1,)), ((), ())), pre...  1.41 us
  transfers between devices with their start and end apart: 1, of which 1 were waited for; matrix products, arithmetic and copies ran while one was open for 2% of the time, Pallas kernels for 0%

profile of v7, /device:TPU:1, one launch (start us, length us, event | category | flops | bytes accessed | tf_op | source)
XLA Modules:
  0.0 66.1 jit_solution(13337692243810110608)
XLA Ops:
  0.6 0.0 copy-start
  0.6 1.6 %encode.1 = (bf16[32,2,16,128]{3,2,1,0:T(8,128)(2,1)S(1)}, s32[16,32]{1,0:T(8,128)S(1)}, s32[8]{0:T(128)S(1)}) custom-call(s32[16,32]{1,0:T(8,128)} %bitcast.7, s32[8]{0:T(128)} %slots_in.1, f32[1,6,128,128]{3,2,1,0:T(8,128)} %master_in.1, bf16[1,6,128,128]{3,2,1,0:T(8,128)(2,1)} %sent_in.1), custom_call_target="tpu_custom_call" | custom-call | tf_op jit(solution)/shard_map/encode/pallas_call | solution.py:165
  2.2 17.8 %all_to_all.15.got = bf16[32,2,16,128]{3,2,1,0:T(8,128)(2,1)S(1)} all-to-all(bf16[32,2,16,128]{3,2,1,0:T(8,128)(2,1)S(1)} %get-tuple-element.7), channel_id=1, replica_groups=mesh['zl'=2,'x'=4,'c'=2,'zh'=4,'ya'=2,'yb'=2,'yc'=2] {'zl','x','c','yc'}, dimensions={0} | all-to-all | bytes 524288 | tf_op jit(solution)/shard_map/all_to_all | solution.py:151
  20.0 0.0 copy-start.1
  20.0 1.1 %slot.1 = bf16[16,2,16,128]{3,2,1,0:T(8,128)(2,1)S(1)} custom-call(s32[16,32]{1,0:T(8,128)S(1)} %get-tuple-element.5.lengths, s32[8]{0:T(128)S(1)} %get-tuple-element.6.slots, bf16[32,2,16,128]{3,2,1,0:T(8,128)(2,1)S(1)} %all_to_all.15.got), custom_call_target="tpu_custom_call" | custom-call | tf_op jit(solution)/shard_map/slot/pallas_call | solution.py:139
  21.1 23.1 %all_to_all.16.got = bf16[16,2,16,128]{3,2,1,0:T(8,128)(2,1)S(1)} all-to-all(bf16[16,2,16,128]{3,2,1,0:T(8,128)(2,1)S(1)} %slot.1), channel_id=1, replica_groups={{0,2,4,6,264,266,268,270,272,274,276,278,24,26,28,30},{1,3,5,7,265,267,..., dimensions={0} | all-to-all | bytes 262144 | tf_op jit(solution)/shard_map/all_to_all | solution.py:188
  44.2 0.1 spread.1
  44.3 13.7 %all_to_all.17.mine = bf16[8,8,3,16,128]{4,3,2,1,0:T(8,128)(2,1)S(1)} all-to-all(bf16[8,8,3,16,128]{4,3,2,1,0:T(8,128)(2,1)S(1)} %spread.1), channel_id=1, replica_groups=mesh['zl'=2,'x'=4,'c'=2,'zh'=4,'ya'=2,'yb'=2,'yc'=2] {'zl','x'}, dimensions={0} | all-to-all | bytes 1572864 | tf_op jit(solution)/shard_map/all_to_all | solution.py:151
  58.1 5.0 %collective-permute-start = (bf16[8,8,3,16,128]{4,3,2,1,0:T(8,128)(2,1)S(1)}, bf16[8,8,3,16,128]{4,3,2,1,0:T(8,128)(2,1)S(1)}, u32[]{:S(2)}, u32[]{:S(2)}) collective-permute-start(bf16[8,8,3,16,128]{4,3,2,1,0:T(8,128)(2,1)S(1)} %all_to_all.17.mine), channel_id=1, source_target_pairs={{0,32},{32,0},{1,33},{33,1},{2,34},{34,2},{3,35},{35,3},{4,36},{36... | collective-permute-start | bytes 2359304 | tf_op jit(solution)/shard_map/ppermute | solution.py:193
  63.0 0.0 copy-done
  63.1 0.0 copy-done.1
  63.1 1.4 %fusion = bf16[1,1,256,384]{3,2,1,0:T(8,128)(2,1)} fusion(bf16[384,2048]{1,0:T(8,128)(2,1)S(1)} %copy-done.1, bf16[1,1,256,2048]{3,2,1,0:T(8,128)(2,1)S(1)} %copy-done), kind=kOutput, calls=%fused_computation.1 | convolution fusion | flops 402751488 | bytes 2818048 | tf_op jit(solution)/shard_map/dot_general | solution.py:194
  64.5 0.2 add_mine.1.new_mine
  64.7 0.2 collective-permute-done.other
  64.9 1.2 %add_other.1 = bf16[384,2048]{1,0:T(8,128)(2,1)} custom-call(bf16[8,8,3,16,128]{4,3,2,1,0:T(8,128)(2,1)S(1)} %collective-permute-done.other, bf16[384,2048]{1,0:T(8,128)(2,1)S(1)} %copy-done.1, bf16[3,64,2048]{2,1,0:T(8,128)(2,1)S(1)} %add_mine.1.new_mine), custom_call_target="tpu_custom_call" | custom-call | tf_op jit(solution)/shard_map/add_other/pallas_call | solution.py:199
Async XLA Ops:
  0.6 62.4 %copy-start = (bf16[1,1,256,2048]{3,2,1,0:T(8,128)(2,1)S(1)}, bf16[1,1,256,2048]{3,2,1,0:T(8,128)(2,1)}, u32[]{:S(2)}) copy-start(bf16[1,1,256,2048]{3,2,1,0:T(8,128)(2,1)} %param.9) | copy-start | bytes 3145732
  20.0 43.1 %copy-start.1 = (bf16[384,2048]{1,0:T(8,128)(2,1)S(1)}, bf16[384,2048]{1,0:T(8,128)(2,1)}, u32[]{:S(2)}) copy-start(bf16[384,2048]{1,0:T(8,128)(2,1)} %base.3) | copy-start | bytes 4718596
  58.1 6.9 %collective-permute-start = (bf16[8,8,3,16,128]{4,3,2,1,0:T(8,128)(2,1)S(1)}, bf16[8,8,3,16,128]{4,3,2,1,0:T(8,128)(2,1)S(1)}, u32[]{:S(2)}, u32[]{:S(2)}) collective-permute-start(bf16[8,8,3,16,128]{4,3,2,1,0:T(8,128)(2,1)S(1)} %all_to_all.17.mine), channel_id=1, source_target_pairs={{0,32},{32,0},{1,33},{33,1},{2,34},{34,2},{3,35},{35,3},{4,36},{36... | collective-permute-start | bytes 2359304 | tf_op jit(solution)/shard_map/ppermute | solution.py:193

commit v8 on v7

--- a/solution.py
+++ b/solution.py
@@ -18,6 +18,10 @@
 MOST = 6
 GROUPS = 16
 EXPERTS = 8
+
+
+def rank_of(col):
+    return col ^ ((col >> 2 & 1) * 3)
 
 
 class Place:
@@ -81,14 +85,15 @@
             kb = odd ^ (i & 1)
             entry = table[e // 4, (e % 4) * TROWS + 6 * kb + 3 * at.yc + i]
             slot = jnp.where((entry & 7) >= (2 if i == 2 else 5), 1, 0)
-            out[2 * p + kb, i >> 1] = got[(entry >> 3) * 2 + e // 4, slot]
+            out[rank_of(2 * p + kb), i >> 1] = got[(entry >> 3) * 2 + e // 4, slot]
 
 
 def spread_kernel(got, out):
     at = Place()
     side = (at.x + at.yb) & 1
     for n in range(8):
-        parts = (got[2 * n + side, 0], got[2 * n + side, 1], got[2 * n + 1 - side, 0])
+        here, there = rank_of(2 * n + side), rank_of(2 * n + 1 - side)
+        parts = (got[here, 0], got[here, 1], got[there, 0])
         for to in range(8):
             for m in range(3):
                 out[to, n, m] = parts[m]
@@ -155,8 +160,11 @@
     sizes = tuple(AXES.values())
     groups = []
     for side, x, c, yc in np.ndindex(2, 4, 2, 2):
-        members = [(side ^ (zh >> 1) ^ (zh & 1), x, c, zh, ya, yb, yc) for zh, ya, yb in np.ndindex(4, 2, 2)]
-        groups.append([int(np.ravel_multi_index(member, sizes)) for member in members])
+        group = [0] * 16
+        for zh, ya, yb in np.ndindex(4, 2, 2):
+            member = (side ^ (zh >> 1) ^ (zh & 1), x, c, zh, ya, yb, yc)
+            group[rank_of(zh * 4 + ya * 2 + yb)] = int(np.ravel_multi_index(member, sizes))
+        groups.append(group)
     return groups
 
 

time: 66.4 us -> 65.6 us (0.988)
  blocking collectives: 54.6 us -> 53.2 us
    all_to_all x2, blocking collectives: 31.5 us -> 30.3 us  [exchange(): return lax.all_to_all(x, axes, split_axis=0, concat_axis=0, tiled=True)]
where the time goes in v8:
time: 65.6 us; the launch traced here: 65.4 us
  blocking collectives  53.2 us (81%)
  starting transfers between devices  5.64 us (9%)
  Pallas kernels  4.23 us (6%)
  matrix products  1.41 us (2%)
  between operations  0.69 us (1%)
    all_to_all x2, blocking collectives, exchange(): return lax.all_to_all(x, axes, split_axis=0, concat_axis=0, tiled=True)  30.3 us
    all_to_all x1, blocking collectives, shards(): lax.all_to_all(out, tuple(AXES), split_axis=0, concat_axis=0, tiled=True,...  22.9 us
    ppermute x1, starting transfers between devices, shards(): other = lax.ppermute(mine, 'c', [(0, 1), (1, 0)])  5.64 us
    pallas_call x1, Pallas kernels, shards(): pl.pallas_call(encode_kernel, out_shape=(jax.ShapeDtypeStruct((32, 2, PAR...  1.58 us
    pallas_call x3, Pallas kernels, call(): pl.pallas_call(kernel, out_shape=outs, in_specs=specs, out_specs=(VMEM,)...  1.47 us
    dot_general x1, matrix products, shards(): lax.dot_general(tokens[0, 0], rollout_base, (((1,), (1,)), ((), ())), pre...  1.41 us
  transfers between devices with their start and end apart: 1, of which 1 were waited for; matrix products, arithmetic and copies ran while one was open for 2% of the time, Pallas kernels for 0%

profile of v8, /device:TPU:1, one launch (start us, length us, event | category | flops | bytes accessed | tf_op | source)
XLA Modules:
  0.0 65.4 jit_solution(18440849975616688905)
XLA Ops:
  0.6 0.0 copy-start
  0.6 1.6 %encode.1 = (bf16[32,2,16,128]{3,2,1,0:T(8,128)(2,1)S(1)}, s32[16,32]{1,0:T(8,128)S(1)}, s32[8]{0:T(128)S(1)}) custom-call(s32[16,32]{1,0:T(8,128)} %bitcast.7, s32[8]{0:T(128)} %slots_in.1, f32[1,6,128,128]{3,2,1,0:T(8,128)} %master_in.1, bf16[1,6,128,128]{3,2,1,0:T(8,128)(2,1)} %sent_in.1), custom_call_target="tpu_custom_call" | custom-call | tf_op jit(solution)/shard_map/encode/pallas_call | solution.py:173
  2.2 17.8 %all_to_all.15.got = bf16[32,2,16,128]{3,2,1,0:T(8,128)(2,1)S(1)} all-to-all(bf16[32,2,16,128]{3,2,1,0:T(8,128)(2,1)S(1)} %get-tuple-element.7), channel_id=1, replica_groups=mesh['zl'=2,'x'=4,'c'=2,'zh'=4,'ya'=2,'yb'=2,'yc'=2] {'zl','x','c','yc'}, dimensions={0} | all-to-all | bytes 524288 | tf_op jit(solution)/shard_map/all_to_all | solution.py:156
  20.0 0.0 copy-start.1
  20.0 1.2 %slot.1 = bf16[16,2,16,128]{3,2,1,0:T(8,128)(2,1)S(1)} custom-call(s32[16,32]{1,0:T(8,128)S(1)} %get-tuple-element.5.lengths, s32[8]{0:T(128)S(1)} %get-tuple-element.6.slots, bf16[32,2,16,128]{3,2,1,0:T(8,128)(2,1)S(1)} %all_to_all.15.got), custom_call_target="tpu_custom_call" | custom-call | tf_op jit(solution)/shard_map/slot/pallas_call | solution.py:144
  21.1 22.9 %all_to_all.16.got = bf16[16,2,16,128]{3,2,1,0:T(8,128)(2,1)S(1)} all-to-all(bf16[16,2,16,128]{3,2,1,0:T(8,128)(2,1)S(1)} %slot.1), channel_id=1, replica_groups={{0,2,4,6,270,268,266,264,272,274,276,278,30,28,26,24},{1,3,5,7,271,269,..., dimensions={0} | all-to-all | bytes 262144 | tf_op jit(solution)/shard_map/all_to_all | solution.py:196
  44.0 0.1 spread.1
  44.2 12.5 %all_to_all.17.mine = bf16[8,8,3,16,128]{4,3,2,1,0:T(8,128)(2,1)S(1)} all-to-all(bf16[8,8,3,16,128]{4,3,2,1,0:T(8,128)(2,1)S(1)} %spread.1), channel_id=1, replica_groups=mesh['zl'=2,'x'=4,'c'=2,'zh'=4,'ya'=2,'yb'=2,'yc'=2] {'zl','x'}, dimensions={0} | all-to-all | bytes 1572864 | tf_op jit(solution)/shard_map/all_to_all | solution.py:156
  56.7 5.6 %collective-permute-start = (bf16[8,8,3,16,128]{4,3,2,1,0:T(8,128)(2,1)S(1)}, bf16[8,8,3,16,128]{4,3,2,1,0:T(8,128)(2,1)S(1)}, u32[]{:S(2)}, u32[]{:S(2)}) collective-permute-start(bf16[8,8,3,16,128]{4,3,2,1,0:T(8,128)(2,1)S(1)} %all_to_all.17.mine), channel_id=1, source_target_pairs={{0,32},{32,0},{1,33},{33,1},{2,34},{34,2},{3,35},{35,3},{4,36},{36... | collective-permute-start | bytes 2359304 | tf_op jit(solution)/shard_map/ppermute | solution.py:201
  62.3 0.0 copy-done
  62.3 0.0 copy-done.1
  62.3 1.4 %fusion = bf16[1,1,256,384]{3,2,1,0:T(8,128)(2,1)} fusion(bf16[384,2048]{1,0:T(8,128)(2,1)S(1)} %copy-done.1, bf16[1,1,256,2048]{3,2,1,0:T(8,128)(2,1)S(1)} %copy-done), kind=kOutput, calls=%fused_computation.1 | convolution fusion | flops 402751488 | bytes 2818048 | tf_op jit(solution)/shard_map/dot_general | solution.py:202
  63.7 0.2 add_mine.1.new_mine
  64.0 0.2 collective-permute-done.other
  64.2 1.2 %add_other.1 = bf16[384,2048]{1,0:T(8,128)(2,1)} custom-call(bf16[8,8,3,16,128]{4,3,2,1,0:T(8,128)(2,1)S(1)} %collective-permute-done.other, bf16[384,2048]{1,0:T(8,128)(2,1)S(1)} %copy-done.1, bf16[3,64,2048]{2,1,0:T(8,128)(2,1)S(1)} %add_mine.1.new_mine), custom_call_target="tpu_custom_call" | custom-call | tf_op jit(solution)/shard_map/add_other/pallas_call | solution.py:207
Async XLA Ops:
  0.6 61.7 %copy-start = (bf16[1,1,256,2048]{3,2,1,0:T(8,128)(2,1)S(1)}, bf16[1,1,256,2048]{3,2,1,0:T(8,128)(2,1)}, u32[]{:S(2)}) copy-start(bf16[1,1,256,2048]{3,2,1,0:T(8,128)(2,1)} %param.9) | copy-start | bytes 3145732
  20.0 42.3 %copy-start.1 = (bf16[384,2048]{1,0:T(8,128)(2,1)S(1)}, bf16[384,2048]{1,0:T(8,128)(2,1)}, u32[]{:S(2)}) copy-start(bf16[384,2048]{1,0:T(8,128)(2,1)} %base.3) | copy-start | bytes 4718596
  56.7 7.5 %collective-permute-start = (bf16[8,8,3,16,128]{4,3,2,1,0:T(8,128)(2,1)S(1)}, bf16[8,8,3,16,128]{4,3,2,1,0:T(8,128)(2,1)S(1)}, u32[]{:S(2)}, u32[]{:S(2)}) collective-permute-start(bf16[8,8,3,16,128]{4,3,2,1,0:T(8,128)(2,1)S(1)} %all_to_all.17.mine), channel_id=1, source_target_pairs={{0,32},{32,0},{1,33},{33,1},{2,34},{34,2},{3,35},{35,3},{4,36},{36... | collective-permute-start | bytes 2359304 | tf_op jit(solution)/shard_map/ppermute | solution.py:201

commit v9 on v7

--- a/solution.py
+++ b/solution.py
@@ -60,7 +60,7 @@
         slot = 0 if j < 2 else 1 if j == 5 else i >> 1
         for n in range(8):
             peer = ((n >> 1 & 1) ^ at.turn) * 16 + (n & 1) * 8 + (n >> 2) * 2
-            out[peer + to, slot] = value[n * PART : (n + 1) * PART, :]
+            out[31 - peer - to, slot] = value[n * PART : (n + 1) * PART, :]
 
     loads[1].wait()
     loads[2].wait()
@@ -81,14 +81,15 @@
             kb = odd ^ (i & 1)
             entry = table[e // 4, (e % 4) * TROWS + 6 * kb + 3 * at.yc + i]
             slot = jnp.where((entry & 7) >= (2 if i == 2 else 5), 1, 0)
-            out[2 * p + kb, i >> 1] = got[(entry >> 3) * 2 + e // 4, slot]
+            out[15 - 2 * p - kb, i >> 1] = got[31 - (entry >> 3) * 2 - e // 4, slot]
 
 
 def spread_kernel(got, out):
     at = Place()
     side = (at.x + at.yb) & 1
     for n in range(8):
-        parts = (got[2 * n + side, 0], got[2 * n + side, 1], got[2 * n + 1 - side, 0])
+        here, there = 15 - 2 * n - side, 14 - 2 * n + side
+        parts = (got[here, 0], got[here, 1], got[there, 0])
         for to in range(8):
             for m in range(3):
                 out[to, n, m] = parts[m]
@@ -100,7 +101,7 @@
         for col in range(16):
             cols = pl.ds(col * BLK, BLK)
             chip = 4 * ((n >> 1) ^ at.turn) + 2 * (n & 1) + ((at.yb + i + col) & 1)
-            part = tiles[chip, col >> 1, (0, 2, 1)[i]].astype(jnp.float32)
+            part = tiles[7 - chip, col >> 1, (0, 2, 1)[i]].astype(jnp.float32)
             new[i, n * PART : (n + 1) * PART, cols] = (base[rows, cols].astype(jnp.float32) + part).astype(jnp.bfloat16)
 
 
@@ -147,17 +148,18 @@
     )(*args)
 
 
-def exchange(x, axes):
-    return lax.all_to_all(x, axes, split_axis=0, concat_axis=0, tiled=True)
-
-
-def turned_groups():
+def exchange(x, names, turn=lambda zh: 0):
     sizes = tuple(AXES.values())
+    rest = [name for name in AXES if name not in names]
     groups = []
-    for side, x, c, yc in np.ndindex(2, 4, 2, 2):
-        members = [(side ^ (zh >> 1) ^ (zh & 1), x, c, zh, ya, yb, yc) for zh, ya, yb in np.ndindex(4, 2, 2)]
-        groups.append([int(np.ravel_multi_index(member, sizes)) for member in members])
-    return groups
+    for fixed in np.ndindex(*(AXES[name] for name in rest)):
+        group = []
+        for moving in np.ndindex(*(AXES[name] for name in names)):
+            at = dict(zip((*rest, *names), fixed + moving))
+            at["zl"] ^= turn(at["zh"])
+            group.append(int(np.ravel_multi_index([at[name] for name in AXES], sizes)))
+        groups.append(group[::-1])
+    return lax.all_to_all(x, tuple(AXES), split_axis=0, concat_axis=0, tiled=True, axis_index_groups=groups)
 
 
 def shards(master_new, sent_base, rollout_base, tokens, lengths, expert_slot):
@@ -185,9 +187,7 @@
         slot_kernel, "slot", [SMEM, SMEM, VMEM], [(16, 2, PART, BLK)], lengths, expert_slot, out,
         scratch=[pltpu.SMEM((2, 64), jnp.int32)],
     )
-    out = lax.all_to_all(
-        out, tuple(AXES), split_axis=0, concat_axis=0, tiled=True, axis_index_groups=turned_groups()
-    )
+    out = exchange(out, ("zh", "ya", "yb"), lambda zh: (zh >> 1) ^ (zh & 1))
     (out,) = call(spread_kernel, "spread", [VMEM], [(8, 8, 3, PART, BLK)], out)
     mine = exchange(out, ("zl", "x"))
     other = lax.ppermute(mine, "c", [(0, 1), (1, 0)])

time: 66.4 us -> 59.8 us (0.901)
  blocking collectives: 54.6 us -> 49.1 us
  starting transfers between devices: 4.98 us -> 3.86 us
    all_to_all x3, blocking collectives: 54.6 us -> 49.1 us  [exchange(): lax.all_to_all(x, tuple(AXES), split_axis=0, concat_axis=0, tiled=True, a...]
    ppermute x1, starting transfers between devices: 4.98 us -> 3.86 us  [shards(): other = lax.ppermute(mine, 'c', [(0, 1), (1, 0)])]
where the time goes in v9:
time: 59.8 us; the launch traced here: 59.6 us
  blocking collectives  49.1 us (82%)
  Pallas kernels  4.25 us (7%)
  starting transfers between devices  3.86 us (6%)
  matrix products  1.41 us (2%)
  between operations  0.7 us (1%)
    all_to_all x3, blocking collectives, exchange(): lax.all_to_all(x, tuple(AXES), split_axis=0, concat_axis=0, tiled=True, a...  49.1 us
    ppermute x1, starting transfers between devices, shards(): other = lax.ppermute(mine, 'c', [(0, 1), (1, 0)])  3.86 us
    pallas_call x1, Pallas kernels, shards(): pl.pallas_call(encode_kernel, out_shape=(jax.ShapeDtypeStruct((32, 2, PAR...  1.58 us
    pallas_call x3, Pallas kernels, call(): pl.pallas_call(kernel, out_shape=outs, in_specs=specs, out_specs=(VMEM,)...  1.48 us
    dot_general x1, matrix products, shards(): lax.dot_general(tokens[0, 0], rollout_base, (((1,), (1,)), ((), ())), pre...  1.41 us
  transfers between devices with their start and end apart: 1, of which 1 were waited for; matrix products, arithmetic and copies ran while one was open for 2% of the time, Pallas kernels for 0%

profile of v9, /device:TPU:1, one launch (start us, length us, event | category | flops | bytes accessed | tf_op | source)
XLA Modules:
  0.0 59.6 jit_solution(5694229107773635808)
XLA Ops:
  0.6 0.0 copy-start
  0.6 1.6 %encode.1 = (bf16[32,2,16,128]{3,2,1,0:T(8,128)(2,1)S(1)}, s32[16,32]{1,0:T(8,128)S(1)}, s32[8]{0:T(128)S(1)}) custom-call(s32[16,32]{1,0:T(8,128)} %bitcast.7, s32[8]{0:T(128)} %slots_in.1, f32[1,6,128,128]{3,2,1,0:T(8,128)} %master_in.1, bf16[1,6,128,128]{3,2,1,0:T(8,128)(2,1)} %sent_in.1), custom_call_target="tpu_custom_call" | custom-call | tf_op jit(solution)/shard_map/encode/pallas_call | solution.py:167
  2.2 17.7 %all_to_all.15.got = bf16[32,2,16,128]{3,2,1,0:T(8,128)(2,1)S(1)} all-to-all(bf16[32,2,16,128]{3,2,1,0:T(8,128)(2,1)S(1)} %get-tuple-element.7), channel_id=1, replica_groups={{481,480,449,448,417,416,385,384,353,352,321,320,289,288,257,256,225,22..., dimensions={0} | all-to-all | bytes 524288 | tf_op jit(solution)/shard_map/all_to_all | solution.py:162
  20.0 0.0 copy-start.1
  20.0 1.2 %slot.1 = bf16[16,2,16,128]{3,2,1,0:T(8,128)(2,1)S(1)} custom-call(s32[16,32]{1,0:T(8,128)S(1)} %get-tuple-element.5.lengths, s32[8]{0:T(128)S(1)} %get-tuple-element.6.slots, bf16[32,2,16,128]{3,2,1,0:T(8,128)(2,1)S(1)} %all_to_all.15.got), custom_call_target="tpu_custom_call" | custom-call | tf_op jit(solution)/shard_map/slot/pallas_call | solution.py:140
  21.1 16.6 %all_to_all.16.got = bf16[16,2,16,128]{3,2,1,0:T(8,128)(2,1)S(1)} all-to-all(bf16[16,2,16,128]{3,2,1,0:T(8,128)(2,1)S(1)} %slot.1), channel_id=1, replica_groups={{30,28,26,24,278,276,274,272,270,268,266,264,6,4,2,0},{31,29,27,25,279,..., dimensions={0} | all-to-all | bytes 262144 | tf_op jit(solution)/shard_map/all_to_all | solution.py:162
  37.7 0.1 spread.1
  37.8 14.8 %all_to_all.17.mine = bf16[8,8,3,16,128]{4,3,2,1,0:T(8,128)(2,1)S(1)} all-to-all(bf16[8,8,3,16,128]{4,3,2,1,0:T(8,128)(2,1)S(1)} %spread.1), channel_id=1, replica_groups={{448,384,320,256,192,128,64,0},{449,385,321,257,193,129,65,1},{450,386,..., dimensions={0} | all-to-all | bytes 1572864 | tf_op jit(solution)/shard_map/all_to_all | solution.py:162
  52.6 3.9 %collective-permute-start = (bf16[8,8,3,16,128]{4,3,2,1,0:T(8,128)(2,1)S(1)}, bf16[8,8,3,16,128]{4,3,2,1,0:T(8,128)(2,1)S(1)}, u32[]{:S(2)}, u32[]{:S(2)}) collective-permute-start(bf16[8,8,3,16,128]{4,3,2,1,0:T(8,128)(2,1)S(1)} %all_to_all.17.mine), channel_id=1, source_target_pairs={{0,32},{32,0},{1,33},{33,1},{2,34},{34,2},{3,35},{35,3},{4,36},{36... | collective-permute-start | bytes 2359304 | tf_op jit(solution)/shard_map/ppermute | solution.py:193
  56.5 0.0 copy-done
  56.5 0.0 copy-done.1
  56.5 1.4 %fusion = bf16[1,1,256,384]{3,2,1,0:T(8,128)(2,1)} fusion(bf16[384,2048]{1,0:T(8,128)(2,1)S(1)} %copy-done.1, bf16[1,1,256,2048]{3,2,1,0:T(8,128)(2,1)S(1)} %copy-done), kind=kOutput, calls=%fused_computation.1 | convolution fusion | flops 402751488 | bytes 2818048 | tf_op jit(solution)/shard_map/dot_general | solution.py:194
  57.9 0.2 add_mine.1.new_mine
  58.2 0.2 collective-permute-done.other
  58.4 1.2 %add_other.1 = bf16[384,2048]{1,0:T(8,128)(2,1)} custom-call(bf16[8,8,3,16,128]{4,3,2,1,0:T(8,128)(2,1)S(1)} %collective-permute-done.other, bf16[384,2048]{1,0:T(8,128)(2,1)S(1)} %copy-done.1, bf16[3,64,2048]{2,1,0:T(8,128)(2,1)S(1)} %add_mine.1.new_mine), custom_call_target="tpu_custom_call" | custom-call | tf_op jit(solution)/shard_map/add_other/pallas_call | solution.py:199
Async XLA Ops:
  0.6 55.9 %copy-start = (bf16[1,1,256,2048]{3,2,1,0:T(8,128)(2,1)S(1)}, bf16[1,1,256,2048]{3,2,1,0:T(8,128)(2,1)}, u32[]{:S(2)}) copy-start(bf16[1,1,256,2048]{3,2,1,0:T(8,128)(2,1)} %param.9) | copy-start | bytes 3145732
  20.0 36.5 %copy-start.1 = (bf16[384,2048]{1,0:T(8,128)(2,1)S(1)}, bf16[384,2048]{1,0:T(8,128)(2,1)}, u32[]{:S(2)}) copy-start(bf16[384,2048]{1,0:T(8,128)(2,1)} %base.3) | copy-start | bytes 4718596
  52.6 5.8 %collective-permute-start = (bf16[8,8,3,16,128]{4,3,2,1,0:T(8,128)(2,1)S(1)}, bf16[8,8,3,16,128]{4,3,2,1,0:T(8,128)(2,1)S(1)}, u32[]{:S(2)}, u32[]{:S(2)}) collective-permute-start(bf16[8,8,3,16,128]{4,3,2,1,0:T(8,128)(2,1)S(1)} %all_to_all.17.mine), channel_id=1, source_target_pairs={{0,32},{32,0},{1,33},{33,1},{2,34},{34,2},{3,35},{35,3},{4,36},{36... | collective-permute-start | bytes 2359304 | tf_op jit(solution)/shard_map/ppermute | solution.py:193

commit v10 on v9

--- a/solution.py
+++ b/solution.py
@@ -56,10 +56,10 @@
         value = (encoded.astype(jnp.float32) * scale).astype(jnp.bfloat16)
         r = lax.rem(start + j, TROWS)
         k, i = lax.div(r, 3), lax.rem(r, 3)
-        to = (((k >> 1) + i + at.yb) & 1) * 4 + (k & 1)
+        to = (((k >> 1) + i + at.yb) & 1) + (k & 1) * 8
         slot = 0 if j < 2 else 1 if j == 5 else i >> 1
         for n in range(8):
-            peer = ((n >> 1 & 1) ^ at.turn) * 16 + (n & 1) * 8 + (n >> 2) * 2
+            peer = (n >> 2) * 16 + ((n >> 1 & 1) ^ at.turn) * 4 + (n & 1) * 2
             out[31 - peer - to, slot] = value[n * PART : (n + 1) * PART, :]
 
     loads[1].wait()
@@ -81,7 +81,7 @@
             kb = odd ^ (i & 1)
             entry = table[e // 4, (e % 4) * TROWS + 6 * kb + 3 * at.yc + i]
             slot = jnp.where((entry & 7) >= (2 if i == 2 else 5), 1, 0)
-            out[15 - 2 * p - kb, i >> 1] = got[31 - (entry >> 3) * 2 - e // 4, slot]
+            out[15 - 2 * p - kb, i >> 1] = got[31 - (entry >> 3 & 1) * 16 - e // 4 * 8 - (entry >> 4), slot]
 
 
 def spread_kernel(got, out):
@@ -182,7 +182,7 @@
         compiler_params=LIMIT,
         name="encode",
     )(*(pltpu.with_memory_space_constraint(v, pltpu.HBM) for v in (lengths, expert_slot, master_new, sent_base)))
-    out = exchange(out, ("zl", "x", "c", "yc"))
+    out = exchange(out, ("c", "yc", "zl", "x"))
     (out,) = call(
         slot_kernel, "slot", [SMEM, SMEM, VMEM], [(16, 2, PART, BLK)], lengths, expert_slot, out,
         scratch=[pltpu.SMEM((2, 64), jnp.int32)],

time: 59.8 us -> 59.4 us (level)
  blocking collectives: 49.1 us -> 48.2 us
    all_to_all x3, blocking collectives: 49.1 us -> 48.2 us  [exchange(): lax.all_to_all(x, tuple(AXES), split_axis=0, concat_axis=0, tiled=True, a...]
where the time goes in v10:
time: 59.4 us; the launch traced here: 59.1 us
  blocking collectives  48.2 us (81%)
  Pallas kernels  4.26 us (7%)
  starting transfers between devices  4.26 us (7%)
  matrix products  1.41 us (2%)
  between operations  0.7 us (1%)
    all_to_all x3, blocking collectives, exchange(): lax.all_to_all(x, tuple(AXES), split_axis=0, concat_axis=0, tiled=True, a...  48.2 us
    ppermute x1, starting transfers between devices, shards(): other = lax.ppermute(mine, 'c', [(0, 1), (1, 0)])  4.26 us
    pallas_call x1, Pallas kernels, shards(): pl.pallas_call(encode_kernel, out_shape=(jax.ShapeDtypeStruct((32, 2, PAR...  1.58 us
    pallas_call x3, Pallas kernels, call(): pl.pallas_call(kernel, out_shape=outs, in_specs=specs, out_specs=(VMEM,)...  1.5 us
    dot_general x1, matrix products, shards(): lax.dot_general(tokens[0, 0], rollout_base, (((1,), (1,)), ((), ())), pre...  1.41 us
  transfers between devices with their start and end apart: 1, of which 1 were waited for; matrix products, arithmetic and copies ran while one was open for 2% of the time, Pallas kernels for 0%

profile of v10, /device:TPU:1, one launch (start us, length us, event | category | flops | bytes accessed | tf_op | source)
XLA Modules:
  0.0 59.1 jit_solution(10995444175562385316)
XLA Ops:
  0.6 0.0 copy-start
  0.6 1.6 %encode.1 = (bf16[32,2,16,128]{3,2,1,0:T(8,128)(2,1)S(1)}, s32[16,32]{1,0:T(8,128)S(1)}, s32[8]{0:T(128)S(1)}) custom-call(s32[16,32]{1,0:T(8,128)} %bitcast.7, s32[8]{0:T(128)} %slots_in.1, f32[1,6,128,128]{3,2,1,0:T(8,128)} %master_in.1, bf16[1,6,128,128]{3,2,1,0:T(8,128)(2,1)} %sent_in.1), custom_call_target="tpu_custom_call" | custom-call | tf_op jit(solution)/shard_map/encode/pallas_call | solution.py:167
  2.2 17.3 %all_to_all.15.got = bf16[32,2,16,128]{3,2,1,0:T(8,128)(2,1)S(1)} all-to-all(bf16[32,2,16,128]{3,2,1,0:T(8,128)(2,1)S(1)} %get-tuple-element.7), channel_id=1, replica_groups={{481,417,353,289,225,161,97,33,480,416,352,288,224,160,96,32,449,385,32..., dimensions={0} | all-to-all | bytes 524288 | tf_op jit(solution)/shard_map/all_to_all | solution.py:162
  19.6 0.0 copy-start.1
  19.6 1.2 %slot.1 = bf16[16,2,16,128]{3,2,1,0:T(8,128)(2,1)S(1)} custom-call(s32[16,32]{1,0:T(8,128)S(1)} %get-tuple-element.5.lengths, s32[8]{0:T(128)S(1)} %get-tuple-element.6.slots, bf16[32,2,16,128]{3,2,1,0:T(8,128)(2,1)S(1)} %all_to_all.15.got), custom_call_target="tpu_custom_call" | custom-call | tf_op jit(solution)/shard_map/slot/pallas_call | solution.py:140
  20.8 16.5 %all_to_all.16.got = bf16[16,2,16,128]{3,2,1,0:T(8,128)(2,1)S(1)} all-to-all(bf16[16,2,16,128]{3,2,1,0:T(8,128)(2,1)S(1)} %slot.1), channel_id=1, replica_groups={{30,28,26,24,278,276,274,272,270,268,266,264,6,4,2,0},{31,29,27,25,279,..., dimensions={0} | all-to-all | bytes 262144 | tf_op jit(solution)/shard_map/all_to_all | solution.py:162
  37.3 0.1 spread.1
  37.4 14.3 %all_to_all.17.mine = bf16[8,8,3,16,128]{4,3,2,1,0:T(8,128)(2,1)S(1)} all-to-all(bf16[8,8,3,16,128]{4,3,2,1,0:T(8,128)(2,1)S(1)} %spread.1), channel_id=1, replica_groups={{448,384,320,256,192,128,64,0},{449,385,321,257,193,129,65,1},{450,386,..., dimensions={0} | all-to-all | bytes 1572864 | tf_op jit(solution)/shard_map/all_to_all | solution.py:162
  51.7 4.3 %collective-permute-start = (bf16[8,8,3,16,128]{4,3,2,1,0:T(8,128)(2,1)S(1)}, bf16[8,8,3,16,128]{4,3,2,1,0:T(8,128)(2,1)S(1)}, u32[]{:S(2)}, u32[]{:S(2)}) collective-permute-start(bf16[8,8,3,16,128]{4,3,2,1,0:T(8,128)(2,1)S(1)} %all_to_all.17.mine), channel_id=1, source_target_pairs={{0,32},{32,0},{1,33},{33,1},{2,34},{34,2},{3,35},{35,3},{4,36},{36... | collective-permute-start | bytes 2359304 | tf_op jit(solution)/shard_map/ppermute | solution.py:193
  56.0 0.0 copy-done
  56.0 0.0 copy-done.1
  56.0 1.4 %fusion = bf16[1,1,256,384]{3,2,1,0:T(8,128)(2,1)} fusion(bf16[384,2048]{1,0:T(8,128)(2,1)S(1)} %copy-done.1, bf16[1,1,256,2048]{3,2,1,0:T(8,128)(2,1)S(1)} %copy-done), kind=kOutput, calls=%fused_computation.1 | convolution fusion | flops 402751488 | bytes 2818048 | tf_op jit(solution)/shard_map/dot_general | solution.py:194
  57.5 0.2 add_mine.1.new_mine
  57.7 0.2 collective-permute-done.other
  57.9 1.2 %add_other.1 = bf16[384,2048]{1,0:T(8,128)(2,1)} custom-call(bf16[8,8,3,16,128]{4,3,2,1,0:T(8,128)(2,1)S(1)} %collective-permute-done.other, bf16[384,2048]{1,0:T(8,128)(2,1)S(1)} %copy-done.1, bf16[3,64,2048]{2,1,0:T(8,128)(2,1)S(1)} %add_mine.1.new_mine), custom_call_target="tpu_custom_call" | custom-call | tf_op jit(solution)/shard_map/add_other/pallas_call | solution.py:199
Async XLA Ops:
  0.6 55.4 %copy-start = (bf16[1,1,256,2048]{3,2,1,0:T(8,128)(2,1)S(1)}, bf16[1,1,256,2048]{3,2,1,0:T(8,128)(2,1)}, u32[]{:S(2)}) copy-start(bf16[1,1,256,2048]{3,2,1,0:T(8,128)(2,1)} %param.9) | copy-start | bytes 3145732
  19.6 36.5 %copy-start.1 = (bf16[384,2048]{1,0:T(8,128)(2,1)S(1)}, bf16[384,2048]{1,0:T(8,128)(2,1)}, u32[]{:S(2)}) copy-start(bf16[384,2048]{1,0:T(8,128)(2,1)} %base.3) | copy-start | bytes 4718596
  51.7 6.2 %collective-permute-start = (bf16[8,8,3,16,128]{4,3,2,1,0:T(8,128)(2,1)S(1)}, bf16[8,8,3,16,128]{4,3,2,1,0:T(8,128)(2,1)S(1)}, u32[]{:S(2)}, u32[]{:S(2)}) collective-permute-start(bf16[8,8,3,16,128]{4,3,2,1,0:T(8,128)(2,1)S(1)} %all_to_all.17.mine), channel_id=1, source_target_pairs={{0,32},{32,0},{1,33},{33,1},{2,34},{34,2},{3,35},{35,3},{4,36},{36... | collective-permute-start | bytes 2359304 | tf_op jit(solution)/shard_map/ppermute | solution.py:193
